TPU v7x, 256 devices: a whole 4x4x8 slice. The times are simulated.
256 devices in a mesh: gx: 16 (over z_hi, x), gy: 16 (over y, z_lo, core).
Axes of the slice: x: 4, y: 4, z: 8 (z_hi: 4, z_lo: 2; z = z_hi * 2 + z_lo), core: 2. Of those that a mesh axis runs over, the one named last changes fastest.
Arguments:
- basis_start: float32 [128, 2048, 256], P('gx', 'gy')
- admit: float32 [128, 2048], P('gx', 'gy'), may hold values from 0.5 to 2
- pattern: int32 [128, 2048], P('gx', 'gy'), may hold values 0 or 1
- ground: float32 [128, 2048], P('gx', 'gy'), may hold values from 0.2 to 2
- capacity: float32 [128, 2048], P('gx', 'gy'), may hold values from 0.5 to 2
- ports: int32 [2048], P(('gx', 'gy')), may hold values from 0 to 1023
- drive: float32 [2048, 64], P(('gx', 'gy')), may hold values from -6 to 6
- corner_table: int32 [32, 3], P('gy'), may hold values from 0 to 3
- level_table: float32 [3, 4], replicated, may hold values from 0.5 to 2
Outputs:
- basis_next: float32 [128, 2048, 256], P('gx', 'gy')
- response: float32 [32, 64, 512], P('gy')
Inputs may be any that keep to these rules, and one draw needn't show every extreme that they name: `ports`: driver d's node index counts row-major inside the tile of 8 x 128 nodes held by device d // 8.
All inputs are finite; a program needn't handle non-finite values. No bound on the sum of `pattern` on one device may be relied on, other than what follows from the above.
Results may differ from a plain program's by a relative error of at most 0.0003.
Values sent between devices are 32-bit elements; how exact they have to be, the bound alone decides.
A program may use at most 64 MiB of HBM per device.

v0:
```python
import functools
import math

import jax
import jax.numpy as jnp
from jax import lax
from jax.experimental import pallas as pl
from jax.experimental.pallas import tpu as pltpu
from jax.sharding import PartitionSpec as P

MESH = pl.DeviceIdType.MESH
highest = lax.Precision.HIGHEST
time_step = 0.25
K = 256
TX = 8
TY = 128
NODES = TX * TY
STEPS = 64
BLOCK = 128
ROWS = 4096


def dot(a, b, ca=1, cb=0, precision=highest):
    return lax.dot_general(
        a, b, (((ca,), (cb,)), ((), ())), precision=precision, preferred_element_type=jnp.float32
    )


def place():
    gx, gy = lax.axis_index("gx"), lax.axis_index("gy")
    z = (gx // 4) * 2 + (gy % 4) // 2
    return gx, gy, gx % 4, gy // 4, z, gy % 2


def device(x, y, z, core):
    return ((z // 2) * 4 + x, y * 4 + (z % 2) * 2 + core)


def stats_kernel(
    basis, admit, pattern, ground, capacity, ports, drive,
    y_out, out,
    strength, sx, left_send, right_send, tiles, halo_row, halo_col,
    top_send, edge_send, next_row, next_col,
    v, got0, got1, got2, got3, send_sem, recv_sem,
):
    gx, gy, x, y, z, core = place()
    up = (lax.rem(gx + 15, 16), gy)
    down = (lax.rem(gx + 1, 16), gy)
    left = (gx, lax.rem(gy + 15, 16))
    right = (gx, lax.rem(gy + 1, 16))
    sibling = device(x, y, z, 1 - core)
    along_x = [device(lax.rem(x + d, 4), y, z, core) for d in range(1, 4)]
    along_y = [device(x, lax.rem(y + d, 4), z, core) for d in range(1, 4)]
    along_z = [device(x, y, lax.rem(z + d, 8), core) for d in range(1, 8)]
    barrier = pltpu.get_barrier_semaphore()
    partners = [up, down, left, right, sibling] + along_x + along_y + along_z
    for partner in partners:
        pl.semaphore_signal(barrier, inc=1, device_id=partner, device_id_type=MESH)

    started = []

    def send(src, dst, target):
        i = len(started)
        copy = pltpu.make_async_remote_copy(
            src_ref=src, dst_ref=dst, send_sem=send_sem.at[i], recv_sem=recv_sem.at[i],
            device_id=target, device_id_type=MESH,
        )
        copy.start()
        started.append(copy)
        return copy

    strength[...] = admit[...] * pattern[...].astype(jnp.float32)
    own = strength[...]
    own_t = own.T
    for r in range(TX):
        rows = pl.ds(r * TY, TY)
        weighted = own_t[:, r : r + 1] * basis[rows, :]
        sx[rows, :] = weighted
        left_send[r : r + 1, :] = weighted[0:1, :]
        right_send[r : r + 1, :] = weighted[TY - 1 : TY, :]
    pl.semaphore_wait(barrier, len(partners))
    last = (TX - 1) * TY
    halo = [
        send(strength, tiles.at[0], down),
        send(strength, tiles.at[1], up),
        send(strength, tiles.at[2], right),
        send(strength, tiles.at[3], left),
        send(sx.at[pl.ds(last, TY), :], halo_row.at[0], down),
        send(sx.at[pl.ds(0, TY), :], halo_row.at[1], up),
        send(right_send, halo_col.at[0], right),
        send(left_send, halo_col.at[1], left),
    ]

    def put(m, value):
        v[pl.ds(m * 512, 256), :] = value[:, :128]
        v[pl.ds(m * 512 + 256, 256), :] = value[:, 128:]

    xt = basis[...].T
    cap = capacity[...]
    cap_t = cap.T
    for r in range(TX):
        rows = pl.ds(r * TY, TY)
        y_out[rows, :] = cap_t[:, r : r + 1] * basis[rows, :]
    put(0, dot(xt, basis[...]))
    put(3, dot(xt, y_out[...]))

    for copy in halo:
        copy.wait_recv()
    has_up, has_down = gx > 0, gx < 15
    has_left, has_right = gy > 0, gy < 15
    above = jnp.where(has_up, tiles[0, TX - 1 : TX, :], 0.0)
    below = jnp.where(has_down, tiles[1, 0:1, :], 0.0)
    before = jnp.where(has_left, tiles[2, :, TY - 1 : TY], 0.0)
    after = jnp.where(has_right, tiles[3, :, 0:1], 0.0)
    degree = (
        jnp.concatenate([above, own[:-1]], 0)
        + jnp.concatenate([own[1:], below], 0)
        + jnp.concatenate([before, own[:, :-1]], 1)
        + jnp.concatenate([own[:, 1:], after], 1)
    )
    diagonal = ground[...] + own * degree
    diagonal_t = diagonal.T
    place_in_row = lax.broadcasted_iota(jnp.int32, (TY, K), 0)

    def moved_back(block, edge):
        return jnp.where(place_in_row == TY - 1, edge, pltpu.roll(block, TY - 1, 0))

    def moved_on(block, edge):
        return jnp.where(place_in_row == 0, edge, pltpu.roll(block, 1, 0))

    halo_up = jnp.where(has_up, halo_row[0], 0.0)
    halo_down = jnp.where(has_down, halo_row[1], 0.0)
    halo_left = jnp.where(has_left, halo_col[0], 0.0)
    halo_right = jnp.where(has_right, halo_col[1], 0.0)
    for r in range(TX):
        rows = pl.ds(r * TY, TY)
        here = sx[rows, :]
        total = moved_on(here, halo_left[r : r + 1]) + moved_back(here, halo_right[r : r + 1])
        total = total + (halo_up if r == 0 else sx[pl.ds((r - 1) * TY, TY), :])
        total = total + (halo_down if r == TX - 1 else sx[pl.ds((r + 1) * TY, TY), :])
        image = diagonal_t[:, r : r + 1] * basis[rows, :] - own_t[:, r : r + 1] * total
        krylov = image / cap_t[:, r : r + 1]
        y_out[rows, :] = krylov
        weighted = own_t[:, r : r + 1] * krylov
        if r == 0:
            top_send[...] = weighted
        edge_send[r : r + 1, :] = weighted[0:1, :]
    border = [send(top_send, next_row, up), send(edge_send, next_col, left)]

    put(1, dot(xt, y_out[...]))
    yt = y_out[...].T
    put(2, dot(yt, y_out[...]))
    cap_y = jnp.concatenate(
        [cap_t[:, r : r + 1] * y_out[pl.ds(r * TY, TY), :] for r in range(TX)], 0
    )
    put(4, dot(xt, cap_y))
    put(5, dot(yt, cap_y))
    node = lax.broadcasted_iota(jnp.int32, (8, NODES), 1)
    driver = lax.broadcasted_iota(jnp.int32, (8, NODES), 0)
    spot = jnp.full((8, NODES), -1, jnp.int32)
    for d in range(8):
        spot = jnp.where(driver == d, ports[d], spot)
    picked = (node == spot).astype(jnp.float32)
    v[pl.ds(3584, 256), 0:STEPS] = dot(dot(picked, basis[...]), drive[...], 0, 0)
    v[pl.ds(3584, 256), STEPS:128] = dot(dot(picked, y_out[...]), drive[...], 0, 0)
    v[pl.ds(3840, 256), :] = jnp.zeros((256, 128), jnp.float32)

    for copy in border:
        copy.wait_recv()
    bottom = jnp.where(has_down, next_row[...], 0.0)
    side = jnp.where(has_right, next_col[...], 0.0)
    for copy in halo:
        copy.wait_send()
    for r in range(TX):
        rows = pl.ds(r * TY, TY)
        here = own_t[:, r : r + 1] * y_out[rows, :]
        sx[rows, :] = here
    for r in range(TX):
        rows = pl.ds(r * TY, TY)
        total = moved_back(sx[rows, :], side[r : r + 1])
        total = total + (bottom if r == TX - 1 else sx[pl.ds((r + 1) * TY, TY), :])
        sx[rows, :] = (
            0.5 * diagonal_t[:, r : r + 1] * y_out[rows, :] - own_t[:, r : r + 1] * total
        )
    put(6, dot(yt, sx[...]))

    mine = core * 2048
    other = (1 - core) * 2048
    a0, b0 = mine, mine + 1024
    a1, b1 = a0 + x * 256, b0 + y * 256
    a2, b2 = a1 + y * 64, b1 + x * 64
    a3, b3 = a2 + z * 8, b2 + z * 8

    def span(ref, start, size):
        return ref.at[pl.ds(pl.multiple_of(start, 8), size), :]

    first = [
        send(span(v, other + h * 1024, 1024), got0.at[h], sibling) for h in range(2)
    ]

    def spread(base, size, line, position, got, ring):
        return [
            send(span(v, base + lax.rem(position + d, ring) * size, size), got.at[d - 1], line[d - 1])
            for d in range(1, ring)
        ]

    def collect(copies, base, size, got, count):
        for copy in copies:
            copy.wait_recv()
        rows = pl.ds(pl.multiple_of(base, 8), size)
        total = v[rows, :]
        for i in range(count):
            total = total + got[i]
        return total

    for h, base in enumerate((a0, b0)):
        first[h].wait_recv()
        rows = pl.ds(pl.multiple_of(base, 8), 1024)
        v[rows, :] = v[rows, :] + got0[h]
        if h == 0:
            one_a = spread(a0, 256, along_x, x, got1.at[0], 4)
        else:
            one_b = spread(b0, 256, along_y, y, got1.at[1], 4)
    v[pl.ds(pl.multiple_of(a1, 8), 256), :] = collect(one_a, a1, 256, got1.at[0], 3)
    two_a = spread(a1, 64, along_y, y, got2.at[0], 4)
    v[pl.ds(pl.multiple_of(b1, 8), 256), :] = collect(one_b, b1, 256, got1.at[1], 3)
    two_b = spread(b1, 64, along_x, x, got2.at[1], 4)
    v[pl.ds(pl.multiple_of(a2, 8), 64), :] = collect(two_a, a2, 64, got2.at[0], 3)
    three_a = spread(a2, 8, along_z, z, got3.at[0], 8)
    v[pl.ds(pl.multiple_of(b2, 8), 64), :] = collect(two_b, b2, 64, got2.at[1], 3)
    three_b = spread(b2, 8, along_z, z, got3.at[1], 8)

    def share(base, size, line):
        return [send(span(out, base, size), span(out, base, size), target) for target in line]

    out[pl.ds(pl.multiple_of(a3, 8), 8), :] = collect(three_a, a3, 8, got3.at[0], 7)
    back_a = share(a3, 8, along_z)
    out[pl.ds(pl.multiple_of(b3, 8), 8), :] = collect(three_b, b3, 8, got3.at[1], 7)
    back_b = share(b3, 8, along_z)
    for copy in back_a:
        copy.wait_recv()
    back_a = share(a2, 64, along_y)
    for copy in back_b:
        copy.wait_recv()
    back_b = share(b2, 64, along_x)
    for copy in back_a:
        copy.wait_recv()
    back_a = share(a1, 256, along_x)
    for copy in back_b:
        copy.wait_recv()
    back_b = share(b1, 256, along_y)
    for copy in back_a:
        copy.wait_recv()
    back_a = share(a0, 1024, [sibling])
    for copy in back_b:
        copy.wait_recv()
    back_b = share(b0, 1024, [sibling])
    for copy in back_a + back_b:
        copy.wait_recv()
    for copy in started[len(halo) :]:
        copy.wait_send()


def stats(basis, admit, pattern, ground, capacity, ports, drive):
    vmem = pl.BlockSpec(memory_space=pltpu.VMEM)
    smem = pl.BlockSpec(memory_space=pltpu.SMEM)
    f32 = jnp.float32
    copies = 8 + 2 + 2 * (2 + 6 + 6 + 14)
    return pl.pallas_call(
        stats_kernel,
        out_shape=(
            jax.ShapeDtypeStruct((NODES, K), f32),
            jax.ShapeDtypeStruct((ROWS, 128), f32),
        ),
        in_specs=[vmem] * 5 + [smem, vmem],
        out_specs=(vmem, vmem),
        scratch_shapes=[
            pltpu.VMEM((TX, TY), f32),
            pltpu.VMEM((NODES, K), f32),
            pltpu.VMEM((TX, K), f32),
            pltpu.VMEM((TX, K), f32),
            pltpu.VMEM((4, TX, TY), f32),
            pltpu.VMEM((2, TY, K), f32),
            pltpu.VMEM((2, TX, K), f32),
            pltpu.VMEM((TY, K), f32),
            pltpu.VMEM((TX, K), f32),
            pltpu.VMEM((TY, K), f32),
            pltpu.VMEM((TX, K), f32),
            pltpu.VMEM((ROWS, 128), f32),
            pltpu.VMEM((2, 1024, 128), f32),
            pltpu.VMEM((2, 3, 256, 128), f32),
            pltpu.VMEM((2, 3, 64, 128), f32),
            pltpu.VMEM((2, 7, 8, 128), f32),
            pltpu.SemaphoreType.DMA((copies,)),
            pltpu.SemaphoreType.DMA((copies,)),
        ],
        compiler_params=pltpu.CompilerParams(
            collective_id=0, has_side_effects=True, vmem_limit_bytes=48 * 1024 * 1024
        ),
        name="stats",
    )(basis, admit, pattern, ground, capacity, ports, drive)


def split(a, count):
    parts = []
    for _ in range(count - 1):
        part = a.astype(jnp.bfloat16)
        parts.append(part)
        a = a - part.astype(jnp.float32)
    return parts + [a.astype(jnp.bfloat16)]


PAIRS = {2: ((0, 0), (0, 1), (1, 0)), 3: ((0, 0), (0, 1), (1, 0), (1, 1), (0, 2), (2, 0))}


def deep_dot(a, b, ca, cb, count=3):
    pairs = PAIRS[count]
    left = jnp.concatenate([a[i] for i, j in pairs], ca)
    right = jnp.concatenate([b[j] for i, j in pairs], cb)
    return lax.dot_general(
        left, right, (((ca,), (cb,)), ((), ())), preferred_element_type=jnp.float32
    )


def sum_dot(a, b, ca=1, cb=0, count=2):
    total = None
    for i, j in PAIRS[count]:
        term = lax.dot_general(
            a[i], b[j], (((ca,), (cb,)), ((), ())), preferred_element_type=jnp.float32
        )
        total = term if total is None else total + term
    return total


def solve_kernel(
    nodes, drivers, sums, corners, levels, next_map, response,
    mats, low_t, cap_mat, forcing, work,
):
    scale = 1.0 / nodes

    def take(m):
        return (
            jnp.concatenate([sums[pl.ds(m * 512, 256), :], sums[pl.ds(m * 512 + 256, 256), :]], 1)
            * scale
        )

    xx, xy, yy, xcx, xcy, ycy, half = [take(m) for m in range(7)]
    mats[0, :256, :256] = xx
    mats[0, :256, 256:] = xy
    mats[0, 256:, 256:] = yy
    cap_mat[:256, :256] = xcx
    cap_mat[:256, 256:] = xcy
    cap_mat[256:, :256] = xcy.T
    cap_mat[256:, 256:] = ycy
    cond_tail = half + half.T
    k = lax.rem(lax.axis_index("gx"), 2)
    g = levels[0, corners[k, 0]]
    ratio = levels[1, corners[k, 1]] * (1.0 / time_step)
    gain = levels[2, corners[k, 2]]
    mats[1, :256, :256] = g * xcy + ratio * xcx
    mats[1, :256, 256:] = g * ycy + ratio * xcy
    mats[1, 256:, 256:] = g * cond_tail + ratio * ycy
    part = sums[pl.ds(3584, 256), :] * (1.0 / math.sqrt(drivers))
    forcing[:256, :] = part[:, :STEPS]
    forcing[256:, :] = part[:, STEPS:]
    for m in range(2):
        mats[m, 256:, :256] = jnp.zeros((256, 256), jnp.float32)

    sub = lax.broadcasted_iota(jnp.int32, (8, 128), 0)
    row_id = lax.broadcasted_iota(jnp.int32, (BLOCK, BLOCK), 0)
    col_id = lax.broadcasted_iota(jnp.int32, (BLOCK, BLOCK), 1)
    eye = (row_id == col_id).astype(jnp.float32)

    def factor_panel(lo):
        rows = [[[work[m, lo + 8 * t : lo + 8 * t + 8, h * 128 : h * 128 + 128] for h in range(2)]
                 for t in range(2)] for m in range(2)]
        cols = [[[jnp.broadcast_to(rows[m][t][0][:, lo + k : lo + k + 1], (8, 128))
                  for k in range(16)] for t in range(2)] for m in range(2)]
        pivots = [[None, None] for m in range(2)]
        for i in range(16):
            own, at = i // 8, i % 8
            for m in range(2):
                col, row = cols[m], rows[m]
                pivot = jnp.broadcast_to(col[own][i][at : at + 1, :], (8, 128))
                inverse = 1.0 / pivot
                saved = pivots[m][own]
                pivots[m][own] = pivot if saved is None else jnp.where(sub == at, pivot, saved)
                below = [
                    jnp.where(sub > at, col[t][i], 0.0) if t == own else col[t][i] for t in range(2)
                ]
                for k in range(i + 1, 16):
                    top = jnp.broadcast_to(col[own][k][at : at + 1, :], (8, 128))
                    for t in range(own, 2):
                        col[t][k] = col[t][k] - (below[t] * top) * inverse
                for h in range(2):
                    top = jnp.broadcast_to(row[own][h][at : at + 1, :], (8, 128))
                    for t in range(own, 2):
                        row[t][h] = row[t][h] - (below[t] * top) * inverse
        done = lo + 16
        for m in range(2):
            root = [lax.rsqrt(pivots[m][t]) for t in range(2)]
            panel = jnp.concatenate(
                [jnp.concatenate([rows[m][t][h] * root[t] for h in range(2)], 1) for t in range(2)],
                0,
            )
            work[m, lo:done, :] = panel
            if done < BLOCK:
                parts = split(panel, 3)
                update = deep_dot([p[:, :BLOCK] for p in parts], parts, 0, 0)
                work[m, done:, :] = work[m, done:, :] - update[done:, :]

    def step(s, carry):
        lo = pl.multiple_of(s * BLOCK, BLOCK)
        for m in range(2):
            work[m, :, :BLOCK] = mats[m, pl.ds(lo, BLOCK), pl.ds(lo, BLOCK)]
            work[m, :, BLOCK:] = eye
        for p in range(BLOCK // 16):
            factor_panel(16 * p)
        low_t[pl.ds(lo, BLOCK), pl.ds(lo, BLOCK)] = jnp.where(
            row_id <= col_id, work[0, :, :BLOCK], 0.0
        )
        for i in range(4):

            @pl.when(s == i)
            def _():
                lo, hi = i * BLOCK, (i + 1) * BLOCK
                for m in range(2):
                    corner = jnp.where(row_id >= col_id, work[m, :, BLOCK:], 0.0)
                    row = deep_dot(split(corner, 3), split(mats[m, lo:hi, :], 3), 1, 0)
                    if i > 0:
                        mats[m, lo:hi, :lo] = row[:, :lo]
                    mats[m, lo:hi, lo:hi] = corner
                    if i < 3:
                        mats[m, lo:hi, hi:] = jnp.zeros((BLOCK, 512 - hi), jnp.float32)
                        if m == 0:
                            low_t[lo:hi, hi:] = row[:, hi:]
                        left = [row[:, :lo]] if i > 0 else []
                        row = jnp.concatenate(left + [corner, row[:, hi:]], 1)
                        parts = split(row, 3)
                        update = deep_dot([p[:, hi:] for p in parts], parts, 0, 0)
                        if i > 0:
                            mats[m, hi:, :lo] = mats[m, hi:, :lo] - update[:, :lo]
                        mats[m, hi:, lo:hi] = -update[:, lo:hi]
                        mats[m, hi:, hi:] = mats[m, hi:, hi:] - update[:, hi:]

        return carry

    low_t[...] = jnp.zeros_like(low_t)
    lax.fori_loop(0, 4, step, 0)

    next_map[...] = mats[0, 256:, :]
    low = split(mats[1], 3)
    half_way = sum_dot(low, split(cap_mat[...] * ratio, 3), 1, 0, 3)
    power = sum_dot(split(half_way, 3), low, 1, 1, 3)
    states = sum_dot(split(forcing[...] * gain, 3), low, 0, 1, 3)
    time = lax.broadcasted_iota(jnp.int32, (STEPS, 512), 0)
    s = 1
    while s < STEPS:
        late = jnp.where(time >= s, pltpu.roll(states, s, 0), 0.0)
        parts = split(power, 2)
        states = states + sum_dot(split(late, 2), parts)
        if 2 * s < STEPS:
            power = sum_dot(parts, parts)
        s *= 2
    states = sum_dot(split(states, 3), low, 1, 0, 3)
    response[...] = sum_dot(split(states, 3), split(low_t[...], 3), 1, 1, 3)


def solve(nodes, drivers, sums, corners, levels):
    vmem = pl.BlockSpec(memory_space=pltpu.VMEM)
    smem = pl.BlockSpec(memory_space=pltpu.SMEM)
    f32 = jnp.float32
    return pl.pallas_call(
        functools.partial(solve_kernel, nodes, drivers),
        out_shape=(
            jax.ShapeDtypeStruct((K, 2 * K), f32),
            jax.ShapeDtypeStruct((STEPS, 2 * K), f32),
        ),
        in_specs=[vmem, smem, smem],
        out_specs=(vmem, vmem),
        scratch_shapes=[
            pltpu.VMEM((2, 512, 512), f32),
            pltpu.VMEM((512, 512), f32),
            pltpu.VMEM((512, 512), f32),
            pltpu.VMEM((512, STEPS), f32),
            pltpu.VMEM((2, BLOCK, 2 * BLOCK), f32),
        ],
        compiler_params=pltpu.CompilerParams(vmem_limit_bytes=48 * 1024 * 1024),
        name="solve",
    )(sums, corners, levels)


def project_kernel(basis, krylov, next_map, second):
    maps = split(next_map[...], 2)
    for c in range(4):
        rows = pl.ds(c * 256, 256)
        second[rows, :] = sum_dot(
            split(basis[rows, :], 2), [m[:, :256] for m in maps], 1, 1
        ) + sum_dot(split(krylov[rows, :], 2), [m[:, 256:] for m in maps], 1, 1)


def project(basis, krylov, next_map):
    vmem = pl.BlockSpec(memory_space=pltpu.VMEM)
    return pl.pallas_call(
        project_kernel,
        out_shape=jax.ShapeDtypeStruct((NODES, K), jnp.float32),
        in_specs=[vmem, vmem, vmem],
        out_specs=vmem,
        compiler_params=pltpu.CompilerParams(vmem_limit_bytes=32 * 1024 * 1024),
        cost_estimate=pl.CostEstimate(
            flops=2 * NODES * 2 * K * K * 3, bytes_accessed=4 * 2**20, transcendentals=0
        ),
        name="project",
    )(basis, krylov, next_map)


def shards(basis_start, admit, pattern, ground, capacity, ports, drive, corner_table, level_table):
    devices = lax.axis_size("gx") * lax.axis_size("gy")
    basis = basis_start.reshape(NODES, K)
    krylov, sums = stats(basis, admit, pattern, ground, capacity, ports, drive)
    next_map, own = solve(
        NODES * devices, ports.shape[0] * devices, sums, corner_table, level_table
    )
    swap = [(i, i ^ 1) for i in range(lax.axis_size("gx"))]
    other = lax.ppermute(own, "gx", swap)
    second = project(basis, krylov, next_map)
    even = lax.rem(lax.axis_index("gx"), 2) == 0
    response = jnp.stack([jnp.where(even, own, other), jnp.where(even, other, own)])
    return second.reshape(TX, TY, K), response


def solution(mesh):
    return jax.shard_map(
        shards,
        mesh=mesh,
        in_specs=(
            P("gx", "gy", None),
            P("gx", "gy"),
            P("gx", "gy"),
            P("gx", "gy"),
            P("gx", "gy"),
            P(("gx", "gy")),
            P(("gx", "gy"), None),
            P("gy", None),
            P(),
        ),
        out_specs=(P("gx", "gy", None), P("gy", None, None)),
        check_vma=False,
    )
```

profile of v0, /device:TPU:1, one launch (start us, length us, event | category | flops | bytes accessed | tf_op | source)
XLA Modules:
  0.0 117.3 jit_solution(8677474462796876840)
XLA Ops:
  0.6 0.0 copy-start
  0.6 1.2 %copy-done = f32[8,128,256]{2,1,0:T(8,128)S(1)} copy-done((f32[8,128,256]{2,1,0:T(8,128)S(1)}, f32[8,128,256]{2,1,0:T(8,128)}, u32[]{:S(2)}) %copy-start) | copy-done | bytes 1048600
  1.9 0.0 copy-start.2
  1.9 0.7 copy-done.2
  2.5 0.0 copy-start.3
  2.5 0.7 copy-done.3
  3.2 0.0 copy-start.4
  3.2 0.7 copy-done.4
  3.9 0.0 copy-start.5
  3.9 0.7 copy-done.5
  4.6 0.0 copy-start.6
  4.6 0.7 copy-done.6
  5.3 0.0 copy-start.9
  5.3 0.7 copy-done.9
  6.0 0.0 copy-start.1
  6.0 67.9 %stats.1 = (f32[1024,256]{1,0:T(8,128)S(1)}, f32[4096,128]{1,0:T(8,128)S(1)}) custom-call(f32[1024,256]{1,0:T(8,128)S(1)} %bitcast.6, f32[8,128]{1,0:T(8,128)S(1)} %copy-done.2, s32[8,128]{1,0:T(8,128)S(1)} %copy-done.3, f32[8,128]{1,0:T(8,128)S(1)} %copy-done.4, f32[8,128]{1,0:T(8,128)S(1)} %copy-done.5, s32[8]{0:T(128)S(1)} %copy-done.9, f32[8,64]{1,0:T(8,128)S(1)} %copy-done.6), custom_call_target="tpu_custom_call" | custom-call | tf_op jit(solution)/shard_map/stats/pallas_call | solution.py:269
  73.9 0.0 copy-start.7
  73.9 0.7 copy-done.7
  74.6 0.0 copy-start.8
  74.6 0.7 copy-done.8
  75.2 36.2 %solve.1 = (f32[256,512]{1,0:T(8,128)S(1)}, f32[64,512]{1,0:T(8,128)S(1)}) custom-call(f32[4096,128]{1,0:T(8,128)S(1)} %get-tuple-element.7.sums, s32[2,3]{1,0:T(2,128)S(1)} %copy-done.8, f32[3,4]{1,0:T(4,128)S(1)} %copy-done.7), custom_call_target="tpu_custom_call" | custom-call | tf_op jit(solution)/shard_map/solve/pallas_call | solution.py:473
  111.4 0.1 collective-permute-start
  111.5 0.0 copy-done.1
  111.5 2.0 %project.1 = f32[1024,256]{1,0:T(8,128)} custom-call(f32[1024,256]{1,0:T(8,128)S(1)} %bitcast.7, f32[1024,256]{1,0:T(8,128)S(1)} %get-tuple-element.6.krylov, f32[256,512]{1,0:T(8,128)S(1)} %get-tuple-element.8.next_map), custom_call_target="tpu_custom_call" | custom-call | flops 805306368 | bytes 4194304 | tf_op jit(solution)/shard_map/project/pallas_call | solution.py:504
  113.5 3.1 %collective-permute-done = f32[64,512]{1,0:T(8,128)S(1)} collective-permute-done((f32[64,512]{1,0:T(8,128)S(1)}, f32[64,512]{1,0:T(8,128)S(1)}, u32[]{:S(2)}, u32[]{:S(2)}) %collective-permute-start) | collective-permute-done | bytes 131104 | tf_op jit(solution)/shard_map/ppermute | solution.py:525
  116.6 0.7 pad_maximum_fusion
  (1 shorter events, 0.0 us)
Async XLA Ops:
  0.6 1.2 %copy-start = (f32[8,128,256]{2,1,0:T(8,128)S(1)}, f32[8,128,256]{2,1,0:T(8,128)}, u32[]{:S(2)}) copy-start(f32[8,128,256]{2,1,0:T(8,128)} %param.9) | copy-start | bytes 3145732
  1.9 0.7 copy-start.2
  2.5 0.7 copy-start.3
  3.2 0.7 copy-start.4
  3.9 0.7 copy-start.5
  4.6 0.7 copy-start.6
  5.3 0.7 copy-start.9
  6.0 105.6 %copy-start.1 = (f32[8,128,256]{2,1,0:T(8,128)S(1)}, f32[8,128,256]{2,1,0:T(8,128)}, u32[]{:S(2)}) copy-start(f32[8,128,256]{2,1,0:T(8,128)} %param.9) | copy-start | bytes 3145732
  73.9 0.7 copy-start.7
  74.6 0.7 copy-start.8
  111.4 5.2 %collective-permute-start = (f32[64,512]{1,0:T(8,128)S(1)}, f32[64,512]{1,0:T(8,128)S(1)}, u32[]{:S(2)}, u32[]{:S(2)}) collective-permute-start(f32[64,512]{1,0:T(8,128)S(1)} %get-tuple-element.9), channel_id=1, source_target_pairs={{0,16},{16,0},{32,48},{48,32},{64,80},{80,64},{96,112},{112,96},{1... | collective-permute-start | bytes 393224 | tf_op jit(solution)/shard_map/ppermute | solution.py:525
where the time goes:
time: 118 us; the launch traced here: 117 us
  Pallas kernels  106 us (90%)
  local copies, waits for them, and re-layouts  6.66 us (6%)
  waiting for transfers between devices  3.05 us (3%)
    pallas_call x1, Pallas kernels, stats(): pl.pallas_call(stats_kernel, out_shape=(jax.ShapeDtypeStruct((NODES, K),...  67.9 us
    pallas_call x1, Pallas kernels, solve(): pl.pallas_call(functools.partial(solve_kernel, nodes, drivers), out_shape...  36.2 us
    unnamed x20, local copies, waits for them, and re-layouts  6.66 us
    ppermute x1, waiting for transfers between devices, shards(): other = lax.ppermute(own, 'gx', swap)  3.05 us
  transfers between devices with their start and end apart: 1, of which 1 were waited for; matrix products, arithmetic and copies ran while one was open for 0% of the time, Pallas kernels for 2%

commit v1 on v0

--- a/solution.py
+++ b/solution.py
@@ -17,7 +17,6 @@
 NODES = TX * TY
 STEPS = 64
 BLOCK = 128
-ROWS = 4096
 
 
 def dot(a, b, ca=1, cb=0, precision=highest):
@@ -36,12 +35,21 @@
     return ((z // 2) * 4 + x, y * 4 + (z % 2) * 2 + core)
 
 
+WAVES = 5
+WAVE = 512
+HALF = 256
+PIECE = 16
+SCALES = 3 * WAVE + 264
+
+
 def stats_kernel(
-    basis, admit, pattern, ground, capacity, ports, drive,
-    y_out, out,
+    basis_in, admit_in, pattern_in, ground_in, capacity_in, ports_in, drive_in,
+    corners_in, levels_in, y_copy, out,
+    basis, admit, pattern, ground, capacity, ports, drive, corners, levels, load_sem,
+    y_out, y_sem,
     strength, sx, left_send, right_send, tiles, halo_row, halo_col,
     top_send, edge_send, next_row, next_col,
-    v, got0, got1, got2, got3, send_sem, recv_sem,
+    v, got_core, got_plane, got_z, send_sem, recv_sem,
 ):
     gx, gy, x, y, z, core = place()
     up = (lax.rem(gx + 15, 16), gy)
@@ -49,13 +57,27 @@
     left = (gx, lax.rem(gy + 15, 16))
     right = (gx, lax.rem(gy + 1, 16))
     sibling = device(x, y, z, 1 - core)
-    along_x = [device(lax.rem(x + d, 4), y, z, core) for d in range(1, 4)]
-    along_y = [device(x, lax.rem(y + d, 4), z, core) for d in range(1, 4)]
+    plane = []
+    for d in range(1, 16):
+        px, py = lax.rem(x + d % 4, 4), lax.rem(y + d // 4, 4)
+        plane.append((px * 4 + py, device(px, py, z, core)))
     along_z = [device(x, y, lax.rem(z + d, 8), core) for d in range(1, 8)]
     barrier = pltpu.get_barrier_semaphore()
-    partners = [up, down, left, right, sibling] + along_x + along_y + along_z
+    partners = [up, down, left, right, sibling] + [p[1] for p in plane] + along_z
     for partner in partners:
         pl.semaphore_signal(barrier, inc=1, device_id=partner, device_id_type=MESH)
+    loads = [
+        pltpu.make_async_copy(src, dst, load_sem.at[i])
+        for i, (src, dst) in enumerate(
+            (
+                (basis_in, basis), (admit_in, admit), (pattern_in, pattern), (ground_in, ground),
+                (capacity_in, capacity), (ports_in, ports), (drive_in, drive),
+                (corners_in, corners), (levels_in, levels),
+            )
+        )
+    ]
+    for copy in loads:
+        copy.start()
 
     started = []
 
@@ -69,15 +91,91 @@
         started.append(copy)
         return copy
 
+    home = x * 4 + y
+    flights = {}
+
+    def span(ref, start, size):
+        return ref.at[pl.ds(pl.multiple_of(start, 8), size), :]
+
+    def start_core(w):
+        start = w * WAVE + (1 - core) * HALF
+        flights[w] = [send(span(v, start, HALF), got_core.at[w], sibling)]
+
+    def landed(w):
+        for copy in flights[w]:
+            copy.wait_recv()
+
+    def start_plane(w):
+        landed(w)
+        start = w * WAVE + core * HALF
+        rows = pl.ds(pl.multiple_of(start, 8), HALF)
+        v[rows, :] = v[rows, :] + got_core[w]
+        flights[w] = [
+            send(span(v, start + spot * PIECE, PIECE), got_plane.at[w, i], target)
+            for i, (spot, target) in enumerate(plane)
+        ]
+
+    def start_z(w):
+        landed(w)
+        start = w * WAVE + core * HALF + home * PIECE
+        total = v[pl.ds(pl.multiple_of(start, 8), PIECE), :]
+        for i in range(15):
+            total = total + got_plane[w, i]
+        got_z[w, z] = total
+        flights[w] = [send(got_z.at[w, z], got_z.at[w, z], target) for target in along_z]
+
+    def start_back(w):
+        landed(w)
+        total = got_z[w, 0]
+        for i in range(1, 8):
+            total = total + got_z[w, i]
+        start = w * WAVE + core * HALF + home * PIECE
+        out[pl.ds(pl.multiple_of(start, 8), PIECE), :] = total
+        flights[w] = [
+            send(span(out, start, PIECE), span(out, start, PIECE), target) for _, target in plane
+        ]
+
+    def start_last(w):
+        landed(w)
+        start = w * WAVE + core * HALF
+        flights[w] = [send(span(out, start, HALF), span(out, start, HALF), sibling)]
+
+    def put(w, value):
+        v[pl.ds(w * WAVE, 256), :] = value[:, :128]
+        v[pl.ds(w * WAVE + 256, 256), :] = value[:, 128:]
+
+    row_id = lax.broadcasted_iota(jnp.int32, (K, K), 0)
+    col_id = lax.broadcasted_iota(jnp.int32, (K, K), 1)
+
+    def put_pair(w, lower, upper):
+        put(w, jnp.where(row_id >= col_id, lower, upper))
+
+    def gram(left_parts, right_parts):
+        return sum_dot(left_parts, right_parts, 1, 0, 4)
+
+    for copy in loads:
+        copy.wait()
     strength[...] = admit[...] * pattern[...].astype(jnp.float32)
     own = strength[...]
     own_t = own.T
+    cap_t = capacity[...].T
     for r in range(TX):
         rows = pl.ds(r * TY, TY)
         weighted = own_t[:, r : r + 1] * basis[rows, :]
         sx[rows, :] = weighted
         left_send[r : r + 1, :] = weighted[0:1, :]
         right_send[r : r + 1, :] = weighted[TY - 1 : TY, :]
+
+    def capped(ref):
+        return jnp.concatenate(
+            [cap_t[:, r : r + 1] * ref[pl.ds(r * TY, TY), :] for r in range(TX)], 0
+        )
+
+    x_parts = split(basis[...], 2)
+    xt_parts = split(basis[...].T, 2)
+    cap_x = capped(basis)
+    put_pair(0, gram(xt_parts, x_parts), gram(xt_parts, split(cap_x, 2)))
+
     pl.semaphore_wait(barrier, len(partners))
     last = (TX - 1) * TY
     halo = [
@@ -90,19 +188,15 @@
         send(right_send, halo_col.at[0], right),
         send(left_send, halo_col.at[1], left),
     ]
-
-    def put(m, value):
-        v[pl.ds(m * 512, 256), :] = value[:, :128]
-        v[pl.ds(m * 512 + 256, 256), :] = value[:, 128:]
-
-    xt = basis[...].T
-    cap = capacity[...]
-    cap_t = cap.T
-    for r in range(TX):
-        rows = pl.ds(r * TY, TY)
-        y_out[rows, :] = cap_t[:, r : r + 1] * basis[rows, :]
-    put(0, dot(xt, basis[...]))
-    put(3, dot(xt, y_out[...]))
+    start_core(0)
+    node = lax.broadcasted_iota(jnp.int32, (8, NODES), 1)
+    driver = lax.broadcasted_iota(jnp.int32, (8, NODES), 0)
+    spot = jnp.full((8, NODES), -1, jnp.int32)
+    for d in range(8):
+        spot = jnp.where(driver == d, ports[d], spot)
+    picked = (node == spot).astype(jnp.float32)
+    v[pl.ds(3 * WAVE, 256), 0:STEPS] = dot(dot(picked, basis[...]), drive[...], 0, 0)
+    start_plane(0)
 
     for copy in halo:
         copy.wait_recv()
@@ -118,8 +212,7 @@
         + jnp.concatenate([before, own[:, :-1]], 1)
         + jnp.concatenate([own[:, 1:], after], 1)
     )
-    diagonal = ground[...] + own * degree
-    diagonal_t = diagonal.T
+    diagonal_t = (ground[...] + own * degree).T
     place_in_row = lax.broadcasted_iota(jnp.int32, (TY, K), 0)
 
     def moved_back(block, edge):
@@ -132,6 +225,7 @@
     halo_down = jnp.where(has_down, halo_row[1], 0.0)
     halo_left = jnp.where(has_left, halo_col[0], 0.0)
     halo_right = jnp.where(has_right, halo_col[1], 0.0)
+    inverse_t = 1.0 / cap_t
     for r in range(TX):
         rows = pl.ds(r * TY, TY)
         here = sx[rows, :]
@@ -139,42 +233,49 @@
         total = total + (halo_up if r == 0 else sx[pl.ds((r - 1) * TY, TY), :])
         total = total + (halo_down if r == TX - 1 else sx[pl.ds((r + 1) * TY, TY), :])
         image = diagonal_t[:, r : r + 1] * basis[rows, :] - own_t[:, r : r + 1] * total
-        krylov = image / cap_t[:, r : r + 1]
+        krylov = image * inverse_t[:, r : r + 1]
         y_out[rows, :] = krylov
         weighted = own_t[:, r : r + 1] * krylov
         if r == 0:
             top_send[...] = weighted
         edge_send[r : r + 1, :] = weighted[0:1, :]
+    y_store = pltpu.make_async_copy(y_out, y_copy, y_sem)
+    y_store.start()
     border = [send(top_send, next_row, up), send(edge_send, next_col, left)]
 
-    put(1, dot(xt, y_out[...]))
-    yt = y_out[...].T
-    put(2, dot(yt, y_out[...]))
-    cap_y = jnp.concatenate(
-        [cap_t[:, r : r + 1] * y_out[pl.ds(r * TY, TY), :] for r in range(TX)], 0
-    )
-    put(4, dot(xt, cap_y))
-    put(5, dot(yt, cap_y))
-    node = lax.broadcasted_iota(jnp.int32, (8, NODES), 1)
-    driver = lax.broadcasted_iota(jnp.int32, (8, NODES), 0)
-    spot = jnp.full((8, NODES), -1, jnp.int32)
-    for d in range(8):
-        spot = jnp.where(driver == d, ports[d], spot)
-    picked = (node == spot).astype(jnp.float32)
-    v[pl.ds(3584, 256), 0:STEPS] = dot(dot(picked, basis[...]), drive[...], 0, 0)
-    v[pl.ds(3584, 256), STEPS:128] = dot(dot(picked, y_out[...]), drive[...], 0, 0)
-    v[pl.ds(3840, 256), :] = jnp.zeros((256, 128), jnp.float32)
+    y_parts = split(y_out[...], 2)
+    put(1, gram(xt_parts, y_parts))
+    start_core(1)
+    cap_y = capped(y_out)
+    v[pl.ds(3 * WAVE, 256), STEPS:128] = dot(dot(picked, y_out[...]), drive[...], 0, 0)
+    v[pl.ds(3 * WAVE + 256, 256), :] = jnp.zeros((256, 128), jnp.float32)
+    for i, squares in enumerate(
+        (basis[...] * cap_x, basis[...] * cap_y, y_out[...] * cap_y)
+    ):
+        along = jnp.sum(squares, axis=0, keepdims=True)
+        v[3 * WAVE + 256 + 2 * i : 3 * WAVE + 257 + 2 * i, :] = along[:, :128]
+        v[3 * WAVE + 257 + 2 * i : 3 * WAVE + 258 + 2 * i, :] = along[:, 128:]
+    start_core(3)
+    start_plane(1)
+    yt_parts = split(y_out[...].T, 2)
+    cap_parts = split(cap_y, 2)
+    cross = gram(xt_parts, cap_parts)
+    put_pair(2, gram(yt_parts, y_parts), 0.5 * (cross + cross.T))
+    start_core(2)
+    start_plane(3)
+    start_z(0)
+    tail = gram(yt_parts, cap_parts)
+    start_plane(2)
 
     for copy in border:
         copy.wait_recv()
+    for copy in halo:
+        copy.wait_send()
     bottom = jnp.where(has_down, next_row[...], 0.0)
     side = jnp.where(has_right, next_col[...], 0.0)
-    for copy in halo:
-        copy.wait_send()
     for r in range(TX):
         rows = pl.ds(r * TY, TY)
-        here = own_t[:, r : r + 1] * y_out[rows, :]
-        sx[rows, :] = here
+        sx[rows, :] = own_t[:, r : r + 1] * y_out[rows, :]
     for r in range(TX):
         rows = pl.ds(r * TY, TY)
         total = moved_back(sx[rows, :], side[r : r + 1])
@@ -182,99 +283,62 @@
         sx[rows, :] = (
             0.5 * diagonal_t[:, r : r + 1] * y_out[rows, :] - own_t[:, r : r + 1] * total
         )
-    put(6, dot(yt, sx[...]))
-
-    mine = core * 2048
-    other = (1 - core) * 2048
-    a0, b0 = mine, mine + 1024
-    a1, b1 = a0 + x * 256, b0 + y * 256
-    a2, b2 = a1 + y * 64, b1 + x * 64
-    a3, b3 = a2 + z * 8, b2 + z * 8
-
-    def span(ref, start, size):
-        return ref.at[pl.ds(pl.multiple_of(start, 8), size), :]
-
-    first = [
-        send(span(v, other + h * 1024, 1024), got0.at[h], sibling) for h in range(2)
-    ]
-
-    def spread(base, size, line, position, got, ring):
-        return [
-            send(span(v, base + lax.rem(position + d, ring) * size, size), got.at[d - 1], line[d - 1])
-            for d in range(1, ring)
-        ]
-
-    def collect(copies, base, size, got, count):
-        for copy in copies:
-            copy.wait_recv()
-        rows = pl.ds(pl.multiple_of(base, 8), size)
-        total = v[rows, :]
-        for i in range(count):
-            total = total + got[i]
-        return total
-
-    for h, base in enumerate((a0, b0)):
-        first[h].wait_recv()
-        rows = pl.ds(pl.multiple_of(base, 8), 1024)
-        v[rows, :] = v[rows, :] + got0[h]
-        if h == 0:
-            one_a = spread(a0, 256, along_x, x, got1.at[0], 4)
-        else:
-            one_b = spread(b0, 256, along_y, y, got1.at[1], 4)
-    v[pl.ds(pl.multiple_of(a1, 8), 256), :] = collect(one_a, a1, 256, got1.at[0], 3)
-    two_a = spread(a1, 64, along_y, y, got2.at[0], 4)
-    v[pl.ds(pl.multiple_of(b1, 8), 256), :] = collect(one_b, b1, 256, got1.at[1], 3)
-    two_b = spread(b1, 64, along_x, x, got2.at[1], 4)
-    v[pl.ds(pl.multiple_of(a2, 8), 64), :] = collect(two_a, a2, 64, got2.at[0], 3)
-    three_a = spread(a2, 8, along_z, z, got3.at[0], 8)
-    v[pl.ds(pl.multiple_of(b2, 8), 64), :] = collect(two_b, b2, 64, got2.at[1], 3)
-    three_b = spread(b2, 8, along_z, z, got3.at[1], 8)
-
-    def share(base, size, line):
-        return [send(span(out, base, size), span(out, base, size), target) for target in line]
-
-    out[pl.ds(pl.multiple_of(a3, 8), 8), :] = collect(three_a, a3, 8, got3.at[0], 7)
-    back_a = share(a3, 8, along_z)
-    out[pl.ds(pl.multiple_of(b3, 8), 8), :] = collect(three_b, b3, 8, got3.at[1], 7)
-    back_b = share(b3, 8, along_z)
-    for copy in back_a:
-        copy.wait_recv()
-    back_a = share(a2, 64, along_y)
-    for copy in back_b:
-        copy.wait_recv()
-    back_b = share(b2, 64, along_x)
-    for copy in back_a:
-        copy.wait_recv()
-    back_a = share(a1, 256, along_x)
-    for copy in back_b:
-        copy.wait_recv()
-    back_b = share(b1, 256, along_y)
-    for copy in back_a:
-        copy.wait_recv()
-    back_a = share(a0, 1024, [sibling])
-    for copy in back_b:
-        copy.wait_recv()
-    back_b = share(b0, 1024, [sibling])
-    for copy in back_a + back_b:
-        copy.wait_recv()
+    start_z(1)
+    half = gram(yt_parts, split(sx[...], 2))
+    put_pair(4, half + half.T, tail)
+    start_core(4)
+    start_back(0)
+    start_z(3)
+    start_plane(4)
+    start_z(2)
+    start_back(1)
+    start_last(0)
+    start_back(3)
+    start_back(2)
+    start_z(4)
+    for w in (1, 3, 2):
+        start_last(w)
+    start_back(4)
+    start_last(4)
+    for w in range(WAVES):
+        landed(w)
+    y_store.wait()
     for copy in started[len(halo) :]:
         copy.wait_send()
-
-
-def stats(basis, admit, pattern, ground, capacity, ports, drive):
+    for kind in range(3):
+        for k in range(2):
+            level = levels[kind, 0]
+            for i in range(1, 4):
+                level = jnp.where(corners[k, kind] == i, levels[kind, i], level)
+            out[SCALES + 2 * kind + k : SCALES + 2 * kind + k + 1, :] = jnp.full((1, 128), level, jnp.float32)
+
+
+def stats(basis, admit, pattern, ground, capacity, ports, drive, corners, levels):
     vmem = pl.BlockSpec(memory_space=pltpu.VMEM)
-    smem = pl.BlockSpec(memory_space=pltpu.SMEM)
+    anywhere = pl.BlockSpec(memory_space=pl.ANY)
     f32 = jnp.float32
-    copies = 8 + 2 + 2 * (2 + 6 + 6 + 14)
+    copies = 8 + 2 + WAVES * (1 + 15 + 7 + 15 + 1)
     return pl.pallas_call(
         stats_kernel,
         out_shape=(
             jax.ShapeDtypeStruct((NODES, K), f32),
-            jax.ShapeDtypeStruct((ROWS, 128), f32),
+            jax.ShapeDtypeStruct((WAVES * WAVE, 128), f32),
         ),
-        in_specs=[vmem] * 5 + [smem, vmem],
-        out_specs=(vmem, vmem),
+        in_specs=[anywhere] * 9,
+        out_specs=(anywhere, vmem),
         scratch_shapes=[
+            pltpu.VMEM((NODES, K), f32),
+            pltpu.VMEM((TX, TY), f32),
+            pltpu.VMEM((TX, TY), jnp.int32),
+            pltpu.VMEM((TX, TY), f32),
+            pltpu.VMEM((TX, TY), f32),
+            pltpu.SMEM((8,), jnp.int32),
+            pltpu.VMEM((8, STEPS), f32),
+            pltpu.SMEM((2, 3), jnp.int32),
+            pltpu.SMEM((3, 4), f32),
+            pltpu.SemaphoreType.DMA((9,)),
+            pltpu.VMEM((NODES, K), f32),
+            pltpu.SemaphoreType.DMA,
             pltpu.VMEM((TX, TY), f32),
             pltpu.VMEM((NODES, K), f32),
             pltpu.VMEM((TX, K), f32),
@@ -286,19 +350,18 @@
             pltpu.VMEM((TX, K), f32),
             pltpu.VMEM((TY, K), f32),
             pltpu.VMEM((TX, K), f32),
-            pltpu.VMEM((ROWS, 128), f32),
-            pltpu.VMEM((2, 1024, 128), f32),
-            pltpu.VMEM((2, 3, 256, 128), f32),
-            pltpu.VMEM((2, 3, 64, 128), f32),
-            pltpu.VMEM((2, 7, 8, 128), f32),
+            pltpu.VMEM((WAVES * WAVE, 128), f32),
+            pltpu.VMEM((WAVES, HALF, 128), f32),
+            pltpu.VMEM((WAVES, 15, PIECE, 128), f32),
+            pltpu.VMEM((WAVES, 8, PIECE, 128), f32),
             pltpu.SemaphoreType.DMA((copies,)),
             pltpu.SemaphoreType.DMA((copies,)),
         ],
         compiler_params=pltpu.CompilerParams(
-            collective_id=0, has_side_effects=True, vmem_limit_bytes=48 * 1024 * 1024
+            collective_id=0, has_side_effects=True, vmem_limit_bytes=65024 * 1024
         ),
         name="stats",
-    )(basis, admit, pattern, ground, capacity, ports, drive)
+    )(basis, admit, pattern, ground, capacity, ports, drive, corners, levels)
 
 
 def split(a, count):
@@ -310,7 +373,11 @@
     return parts + [a.astype(jnp.bfloat16)]
 
 
-PAIRS = {2: ((0, 0), (0, 1), (1, 0)), 3: ((0, 0), (0, 1), (1, 0), (1, 1), (0, 2), (2, 0))}
+PAIRS = {
+    2: ((0, 0), (0, 1), (1, 0)),
+    4: ((0, 0), (0, 1), (1, 0), (1, 1)),
+    3: ((0, 0), (0, 1), (1, 0), (1, 1), (0, 2), (2, 0)),
+}
 
 
 def deep_dot(a, b, ca, cb, count=3):
@@ -333,34 +400,55 @@
 
 
 def solve_kernel(
-    nodes, drivers, sums, corners, levels, next_map, response,
+    nodes, drivers, sums, next_map, response,
     mats, low_t, cap_mat, forcing, work,
 ):
     scale = 1.0 / nodes
 
-    def take(m):
+    row_id = lax.broadcasted_iota(jnp.int32, (K, K), 0)
+    col_id = lax.broadcasted_iota(jnp.int32, (K, K), 1)
+
+    def take(w):
+        start = w * WAVE
         return (
-            jnp.concatenate([sums[pl.ds(m * 512, 256), :], sums[pl.ds(m * 512 + 256, 256), :]], 1)
+            jnp.concatenate([sums[pl.ds(start, 256), :], sums[pl.ds(start + 256, 256), :]], 1)
             * scale
         )
 
-    xx, xy, yy, xcx, xcy, ycy, half = [take(m) for m in range(7)]
+    def take_pair(w, place):
+        both = take(w)
+        turned = both.T
+        at = 3 * WAVE + 256 + 2 * place
+        diag = jnp.concatenate([sums[at : at + 1, :], sums[at + 1 : at + 2, :]], 1) * scale
+        lower = jnp.where(row_id >= col_id, both, turned)
+        upper = jnp.where(row_id < col_id, both, jnp.where(row_id == col_id, diag, turned))
+        return lower, upper
+
+    xx, xcx = take_pair(0, 0)
+    xy = take(1)
+    yy, xcy = take_pair(2, 1)
+    cond_tail, ycy = take_pair(4, 2)
     mats[0, :256, :256] = xx
     mats[0, :256, 256:] = xy
     mats[0, 256:, 256:] = yy
     cap_mat[:256, :256] = xcx
     cap_mat[:256, 256:] = xcy
-    cap_mat[256:, :256] = xcy.T
+    cap_mat[256:, :256] = xcy
     cap_mat[256:, 256:] = ycy
-    cond_tail = half + half.T
     k = lax.rem(lax.axis_index("gx"), 2)
-    g = levels[0, corners[k, 0]]
-    ratio = levels[1, corners[k, 1]] * (1.0 / time_step)
-    gain = levels[2, corners[k, 2]]
+    g, ratio, gain = [
+        jnp.where(
+            k == 0,
+            sums[SCALES + 2 * i : SCALES + 2 * i + 1, 0:1],
+            sums[SCALES + 2 * i + 1 : SCALES + 2 * i + 2, 0:1],
+        )
+        for i in range(3)
+    ]
+    ratio = ratio * (1.0 / time_step)
     mats[1, :256, :256] = g * xcy + ratio * xcx
     mats[1, :256, 256:] = g * ycy + ratio * xcy
     mats[1, 256:, 256:] = g * cond_tail + ratio * ycy
-    part = sums[pl.ds(3584, 256), :] * (1.0 / math.sqrt(drivers))
+    part = sums[pl.ds(3 * WAVE, 256), :] * (1.0 / math.sqrt(drivers))
     forcing[:256, :] = part[:, :STEPS]
     forcing[256:, :] = part[:, STEPS:]
     for m in range(2):
@@ -458,17 +546,22 @@
     while s < STEPS:
         late = jnp.where(time >= s, pltpu.roll(states, s, 0), 0.0)
         parts = split(power, 2)
-        states = states + sum_dot(split(late, 2), parts)
+        late_parts = split(late, 2)
         if 2 * s < STEPS:
-            power = sum_dot(parts, parts)
+            both = sum_dot(
+                [jnp.concatenate([p, q], 0) for p, q in zip(parts, late_parts)], parts
+            )
+            power = both[:512]
+            states = states + both[512:]
+        else:
+            states = states + sum_dot(late_parts, parts)
         s *= 2
     states = sum_dot(split(states, 3), low, 1, 0, 3)
     response[...] = sum_dot(split(states, 3), split(low_t[...], 3), 1, 1, 3)
 
 
-def solve(nodes, drivers, sums, corners, levels):
+def solve(nodes, drivers, sums):
     vmem = pl.BlockSpec(memory_space=pltpu.VMEM)
-    smem = pl.BlockSpec(memory_space=pltpu.SMEM)
     f32 = jnp.float32
     return pl.pallas_call(
         functools.partial(solve_kernel, nodes, drivers),
@@ -476,7 +569,7 @@
             jax.ShapeDtypeStruct((K, 2 * K), f32),
             jax.ShapeDtypeStruct((STEPS, 2 * K), f32),
         ),
-        in_specs=[vmem, smem, smem],
+        in_specs=[vmem],
         out_specs=(vmem, vmem),
         scratch_shapes=[
             pltpu.VMEM((2, 512, 512), f32),
@@ -487,7 +580,7 @@
         ],
         compiler_params=pltpu.CompilerParams(vmem_limit_bytes=48 * 1024 * 1024),
         name="solve",
-    )(sums, corners, levels)
+    )(sums)
 
 
 def project_kernel(basis, krylov, next_map, second):
@@ -517,9 +610,11 @@
 def shards(basis_start, admit, pattern, ground, capacity, ports, drive, corner_table, level_table):
     devices = lax.axis_size("gx") * lax.axis_size("gy")
     basis = basis_start.reshape(NODES, K)
-    krylov, sums = stats(basis, admit, pattern, ground, capacity, ports, drive)
+    krylov, sums = stats(
+        basis, admit, pattern, ground, capacity, ports, drive, corner_table, level_table
+    )
     next_map, own = solve(
-        NODES * devices, ports.shape[0] * devices, sums, corner_table, level_table
+        NODES * devices, ports.shape[0] * devices, sums
     )
     swap = [(i, i ^ 1) for i in range(lax.axis_size("gx"))]
     other = lax.ppermute(own, "gx", swap)

time: 118 us -> 97.5 us (0.83)
  Pallas kernels: 106 us -> 91.2 us
  local copies, waits for them, and re-layouts: 6.66 us -> 2.63 us
  waiting for transfers between devices: 3.05 us -> 1.86 us
    pallas_call x1, Pallas kernels: 67.9 us -> 54.7 us  [stats(): pl.pallas_call(stats_kernel, out_shape=(jax.ShapeDtypeStruct((NODES, K),...]
    unnamed x20 -> x6, local copies, waits for them, and re-layouts: 6.66 us -> 2.63 us
    pallas_call x1, Pallas kernels: 36.2 us -> 34.5 us  [solve(): pl.pallas_call(functools.partial(solve_kernel, nodes, drivers), out_shape...]
    ppermute x1, waiting for transfers between devices: 3.05 us -> 1.86 us  [shards(): other = lax.ppermute(own, 'gx', swap)]
where the time goes in v1:
time: 97.5 us; the launch traced here: 97.3 us
  Pallas kernels  91.2 us (94%)
  local copies, waits for them, and re-layouts  2.63 us (3%)
  waiting for transfers between devices  1.86 us (2%)
    pallas_call x1, Pallas kernels, stats(): pl.pallas_call(stats_kernel, out_shape=(jax.ShapeDtypeStruct((NODES, K),...  54.7 us
    pallas_call x1, Pallas kernels, solve(): pl.pallas_call(functools.partial(solve_kernel, nodes, drivers), out_shape...  34.5 us
    unnamed x6, local copies, waits for them, and re-layouts  2.63 us
    pallas_call x1, Pallas kernels, project(): pl.pallas_call(project_kernel, out_shape=jax.ShapeDtypeStruct((NODES, K),...  1.98 us
  transfers between devices with their start and end apart: 1, of which 1 were waited for; matrix products, arithmetic and copies ran while one was open for 0% of the time, Pallas kernels for 2%

profile of v1, /device:TPU:1, one launch (start us, length us, event | category | flops | bytes accessed | tf_op | source)
XLA Modules:
  0.0 97.3 jit_solution(14560068967171370177)
XLA Ops:
  0.6 54.7 %stats.1 = (f32[1024,256]{1,0:T(8,128)}, f32[2560,128]{1,0:T(8,128)}) custom-call(f32[1024,256]{1,0:T(8,128)} %bitcast.6, f32[8,128]{1,0:T(8,128)} %admit_in.1, s32[8,128]{1,0:T(8,128)} %pattern_in.1, f32[8,128]{1,0:T(8,128)} %ground_in.1, f32[8,128]{1,0:T(8,128)} %capacity_in.1, s32[8]{0:T(128)} %ports_in.1, f32[8,64]{1,0:T(8,128)} %drive_in.1, ...), custom_call_target="tpu_custom_call" | custom-call | tf_op jit(solution)/shard_map/stats/pallas_call | solution.py:321
  55.4 0.0 copy-start
  55.4 0.0 copy-start.1
  55.4 1.4 %copy-done.1 = f32[2560,128]{1,0:T(8,128)S(1)} copy-done((f32[2560,128]{1,0:T(8,128)S(1)}, f32[2560,128]{1,0:T(8,128)}, u32[]{:S(2)}) %copy-start.1) | copy-done | bytes 1310744
  56.8 34.5 %solve.1 = (f32[256,512]{1,0:T(8,128)S(1)}, f32[64,512]{1,0:T(8,128)S(1)}) custom-call(f32[2560,128]{1,0:T(8,128)S(1)} %copy-done.1), custom_call_target="tpu_custom_call" | custom-call | tf_op jit(solution)/shard_map/solve/pallas_call | solution.py:566
  91.3 0.2 collective-permute-start
  91.5 0.0 copy-done
  91.5 0.0 copy-start.2
  91.5 1.2 %copy-done.2 = f32[1024,256]{1,0:T(8,128)S(1)} copy-done((f32[1024,256]{1,0:T(8,128)S(1)}, f32[1024,256]{1,0:T(8,128)}, u32[]{:S(2)}) %copy-start.2) | copy-done | bytes 1048600
  92.7 2.0 %project.1 = f32[1024,256]{1,0:T(8,128)} custom-call(f32[1024,256]{1,0:T(8,128)S(1)} %bitcast.7, f32[1024,256]{1,0:T(8,128)S(1)} %copy-done.2, f32[256,512]{1,0:T(8,128)S(1)} %get-tuple-element.8.next_map), custom_call_target="tpu_custom_call" | custom-call | flops 805306368 | bytes 4194304 | tf_op jit(solution)/shard_map/project/pallas_call | solution.py:597
  94.7 1.9 %collective-permute-done = f32[64,512]{1,0:T(8,128)S(1)} collective-permute-done((f32[64,512]{1,0:T(8,128)S(1)}, f32[64,512]{1,0:T(8,128)S(1)}, u32[]{:S(2)}, u32[]{:S(2)}) %collective-permute-start) | collective-permute-done | bytes 131104 | tf_op jit(solution)/shard_map/ppermute | solution.py:620
  96.6 0.7 pad_maximum_fusion
  (1 shorter events, 0.0 us)
Async XLA Ops:
  55.4 36.2 %copy-start = (f32[8,128,256]{2,1,0:T(8,128)S(1)}, f32[8,128,256]{2,1,0:T(8,128)}, u32[]{:S(2)}) copy-start(f32[8,128,256]{2,1,0:T(8,128)} %param.9) | copy-start | bytes 3145732
  55.4 1.4 %copy-start.1 = (f32[2560,128]{1,0:T(8,128)S(1)}, f32[2560,128]{1,0:T(8,128)}, u32[]{:S(2)}) copy-start(f32[2560,128]{1,0:T(8,128)} %get-tuple-element.7.sums) | copy-start | bytes 3932164
  91.3 5.3 %collective-permute-start = (f32[64,512]{1,0:T(8,128)S(1)}, f32[64,512]{1,0:T(8,128)S(1)}, u32[]{:S(2)}, u32[]{:S(2)}) collective-permute-start(f32[64,512]{1,0:T(8,128)S(1)} %get-tuple-element.9), channel_id=1, source_target_pairs={{0,16},{16,0},{32,48},{48,32},{64,80},{80,64},{96,112},{112,96},{1... | collective-permute-start | bytes 393224 | tf_op jit(solution)/shard_map/ppermute | solution.py:620
  91.5 1.2 %copy-start.2 = (f32[1024,256]{1,0:T(8,128)S(1)}, f32[1024,256]{1,0:T(8,128)}, u32[]{:S(2)}) copy-start(f32[1024,256]{1,0:T(8,128)} %get-tuple-element.6.krylov) | copy-start | bytes 3145732

commit v2 on v1

--- a/solution.py
+++ b/solution.py
@@ -44,12 +44,13 @@
 
 def stats_kernel(
     basis_in, admit_in, pattern_in, ground_in, capacity_in, ports_in, drive_in,
-    corners_in, levels_in, y_copy, out,
+    corners_in, levels_in, y_copy, next_map, response, out,
     basis, admit, pattern, ground, capacity, ports, drive, corners, levels, load_sem,
     y_out, y_sem,
     strength, sx, left_send, right_send, tiles, halo_row, halo_col,
     top_send, edge_send, next_row, next_col,
-    v, got_core, got_plane, got_z, send_sem, recv_sem,
+    v, got_core, got_plane, got_z, send_sem, recv_sem, mats, low_t, cap_mat, forcing, work,
+    *, nodes, drivers,
 ):
     gx, gy, x, y, z, core = place()
     up = (lax.rem(gx + 15, 16), gy)
@@ -58,10 +59,10 @@
     right = (gx, lax.rem(gy + 1, 16))
     sibling = device(x, y, z, 1 - core)
     plane = []
-    for d in range(1, 16):
+    for d in sorted(range(1, 16), key=lambda d: -min(d % 4, 4 - d % 4) - min(d // 4, 4 - d // 4)):
         px, py = lax.rem(x + d % 4, 4), lax.rem(y + d // 4, 4)
         plane.append((px * 4 + py, device(px, py, z, core)))
-    along_z = [device(x, y, lax.rem(z + d, 8), core) for d in range(1, 8)]
+    along_z = [device(x, y, lax.rem(z + d, 8), core) for d in (4, 3, 5, 2, 6, 1, 7)]
     barrier = pltpu.get_barrier_semaphore()
     partners = [up, down, left, right, sibling] + [p[1] for p in plane] + along_z
     for partner in partners:
@@ -311,22 +312,27 @@
             for i in range(1, 4):
                 level = jnp.where(corners[k, kind] == i, levels[kind, i], level)
             out[SCALES + 2 * kind + k : SCALES + 2 * kind + k + 1, :] = jnp.full((1, 128), level, jnp.float32)
-
-
-def stats(basis, admit, pattern, ground, capacity, ports, drive, corners, levels):
+    solve_sums(
+        nodes, drivers, out, next_map, response, mats, low_t, cap_mat, forcing, work
+    )
+
+
+def stats(nodes, drivers, basis, admit, pattern, ground, capacity, ports, drive, corners, levels):
     vmem = pl.BlockSpec(memory_space=pltpu.VMEM)
     anywhere = pl.BlockSpec(memory_space=pl.ANY)
     f32 = jnp.float32
     copies = 8 + 2 + WAVES * (1 + 15 + 7 + 15 + 1)
     return pl.pallas_call(
-        stats_kernel,
+        functools.partial(stats_kernel, nodes=nodes, drivers=drivers),
         out_shape=(
             jax.ShapeDtypeStruct((NODES, K), f32),
-            jax.ShapeDtypeStruct((WAVES * WAVE, 128), f32),
+            jax.ShapeDtypeStruct((K, 2 * K), f32),
+            jax.ShapeDtypeStruct((STEPS, 2 * K), f32),
         ),
         in_specs=[anywhere] * 9,
-        out_specs=(anywhere, vmem),
+        out_specs=(anywhere, vmem, vmem),
         scratch_shapes=[
+            pltpu.VMEM((WAVES * WAVE, 128), f32),
             pltpu.VMEM((NODES, K), f32),
             pltpu.VMEM((TX, TY), f32),
             pltpu.VMEM((TX, TY), jnp.int32),
@@ -356,6 +362,11 @@
             pltpu.VMEM((WAVES, 8, PIECE, 128), f32),
             pltpu.SemaphoreType.DMA((copies,)),
             pltpu.SemaphoreType.DMA((copies,)),
+            pltpu.VMEM((2, 512, 512), f32),
+            pltpu.VMEM((512, 512), f32),
+            pltpu.VMEM((512, 512), f32),
+            pltpu.VMEM((512, STEPS), f32),
+            pltpu.VMEM((2, BLOCK, 2 * BLOCK), f32),
         ],
         compiler_params=pltpu.CompilerParams(
             collective_id=0, has_side_effects=True, vmem_limit_bytes=65024 * 1024
@@ -399,7 +410,7 @@
     return total
 
 
-def solve_kernel(
+def solve_sums(
     nodes, drivers, sums, next_map, response,
     mats, low_t, cap_mat, forcing, work,
 ):
@@ -459,38 +470,44 @@
     col_id = lax.broadcasted_iota(jnp.int32, (BLOCK, BLOCK), 1)
     eye = (row_id == col_id).astype(jnp.float32)
 
+    def eliminate(rows, lo, first):
+        tiles = range(first, 4)
+        at = lo + 8 * first
+        cols = {
+            t: [jnp.broadcast_to(rows[t][0][:, at + k : at + k + 1], (8, 128)) for k in range(8)]
+            for t in tiles
+        }
+        pivots = None
+        for i in range(8):
+            pivot = jnp.broadcast_to(cols[first][i][i : i + 1, :], (8, 128))
+            inverse = 1.0 / pivot
+            pivots = pivot if pivots is None else jnp.where(sub == i, pivot, pivots)
+            below = {t: cols[t][i] * inverse for t in tiles}
+            below[first] = jnp.where(sub > i, below[first], 0.0)
+            for k in range(i + 1, 8):
+                top = jnp.broadcast_to(cols[first][k][i : i + 1, :], (8, 128))
+                for t in tiles:
+                    cols[t][k] = cols[t][k] - below[t] * top
+            for h in range(2):
+                top = jnp.broadcast_to(rows[first][h][i : i + 1, :], (8, 128))
+                for t in tiles:
+                    rows[t][h] = rows[t][h] - below[t] * top
+        root = lax.rsqrt(pivots)
+        return [rows[first][h] * root for h in range(2)]
+
     def factor_panel(lo):
-        rows = [[[work[m, lo + 8 * t : lo + 8 * t + 8, h * 128 : h * 128 + 128] for h in range(2)]
-                 for t in range(2)] for m in range(2)]
-        cols = [[[jnp.broadcast_to(rows[m][t][0][:, lo + k : lo + k + 1], (8, 128))
-                  for k in range(16)] for t in range(2)] for m in range(2)]
-        pivots = [[None, None] for m in range(2)]
-        for i in range(16):
-            own, at = i // 8, i % 8
+        done = lo + 32
+        rows = [
+            [[work[m, lo + 8 * t : lo + 8 * t + 8, h * 128 : h * 128 + 128] for h in range(2)]
+             for t in range(4)]
+            for m in range(2)
+        ]
+        final = [[None] * 4, [None] * 4]
+        for t in range(4):
             for m in range(2):
-                col, row = cols[m], rows[m]
-                pivot = jnp.broadcast_to(col[own][i][at : at + 1, :], (8, 128))
-                inverse = 1.0 / pivot
-                saved = pivots[m][own]
-                pivots[m][own] = pivot if saved is None else jnp.where(sub == at, pivot, saved)
-                below = [
-                    jnp.where(sub > at, col[t][i], 0.0) if t == own else col[t][i] for t in range(2)
-                ]
-                for k in range(i + 1, 16):
-                    top = jnp.broadcast_to(col[own][k][at : at + 1, :], (8, 128))
-                    for t in range(own, 2):
-                        col[t][k] = col[t][k] - (below[t] * top) * inverse
-                for h in range(2):
-                    top = jnp.broadcast_to(row[own][h][at : at + 1, :], (8, 128))
-                    for t in range(own, 2):
-                        row[t][h] = row[t][h] - (below[t] * top) * inverse
-        done = lo + 16
+                final[m][t] = eliminate(rows[m], lo, t)
         for m in range(2):
-            root = [lax.rsqrt(pivots[m][t]) for t in range(2)]
-            panel = jnp.concatenate(
-                [jnp.concatenate([rows[m][t][h] * root[t] for h in range(2)], 1) for t in range(2)],
-                0,
-            )
+            panel = jnp.concatenate([jnp.concatenate(final[m][t], 1) for t in range(4)], 0)
             work[m, lo:done, :] = panel
             if done < BLOCK:
                 parts = split(panel, 3)
@@ -502,8 +519,8 @@
         for m in range(2):
             work[m, :, :BLOCK] = mats[m, pl.ds(lo, BLOCK), pl.ds(lo, BLOCK)]
             work[m, :, BLOCK:] = eye
-        for p in range(BLOCK // 16):
-            factor_panel(16 * p)
+        for p in range(BLOCK // 32):
+            factor_panel(32 * p)
         low_t[pl.ds(lo, BLOCK), pl.ds(lo, BLOCK)] = jnp.where(
             row_id <= col_id, work[0, :, :BLOCK], 0.0
         )
@@ -537,10 +554,10 @@
     lax.fori_loop(0, 4, step, 0)
 
     next_map[...] = mats[0, 256:, :]
-    low = split(mats[1], 3)
-    half_way = sum_dot(low, split(cap_mat[...] * ratio, 3), 1, 0, 3)
-    power = sum_dot(split(half_way, 3), low, 1, 1, 3)
-    states = sum_dot(split(forcing[...] * gain, 3), low, 0, 1, 3)
+    low = split(mats[1], 2)
+    half_way = sum_dot(low, split(cap_mat[...] * ratio, 2))
+    power = sum_dot(split(half_way, 2), low, 1, 1)
+    states = sum_dot(split(forcing[...] * gain, 2), low, 0, 1)
     time = lax.broadcasted_iota(jnp.int32, (STEPS, 512), 0)
     s = 1
     while s < STEPS:
@@ -556,35 +573,23 @@
         else:
             states = states + sum_dot(late_parts, parts)
         s *= 2
-    states = sum_dot(split(states, 3), low, 1, 0, 3)
-    response[...] = sum_dot(split(states, 3), split(low_t[...], 3), 1, 1, 3)
-
-
-def solve(nodes, drivers, sums):
-    vmem = pl.BlockSpec(memory_space=pltpu.VMEM)
-    f32 = jnp.float32
-    return pl.pallas_call(
-        functools.partial(solve_kernel, nodes, drivers),
-        out_shape=(
-            jax.ShapeDtypeStruct((K, 2 * K), f32),
-            jax.ShapeDtypeStruct((STEPS, 2 * K), f32),
-        ),
-        in_specs=[vmem],
-        out_specs=(vmem, vmem),
-        scratch_shapes=[
-            pltpu.VMEM((2, 512, 512), f32),
-            pltpu.VMEM((512, 512), f32),
-            pltpu.VMEM((512, 512), f32),
-            pltpu.VMEM((512, STEPS), f32),
-            pltpu.VMEM((2, BLOCK, 2 * BLOCK), f32),
-        ],
-        compiler_params=pltpu.CompilerParams(vmem_limit_bytes=48 * 1024 * 1024),
-        name="solve",
-    )(sums)
-
-
-def project_kernel(basis, krylov, next_map, second):
+    states = sum_dot(split(states, 2), low)
+    response[...] = sum_dot(split(states, 2), split(low_t[...], 2), 1, 1)
+
+
+def project_kernel(basis_in, krylov_in, next_map_in, second, basis, krylov, next_map, load_sem):
+    loads = [
+        pltpu.make_async_copy(src, dst, load_sem.at[i])
+        for i, (src, dst) in enumerate(
+            ((next_map_in, next_map), (basis_in, basis), (krylov_in, krylov))
+        )
+    ]
+    for copy in loads:
+        copy.start()
+    loads[0].wait()
     maps = split(next_map[...], 2)
+    loads[1].wait()
+    loads[2].wait()
     for c in range(4):
         rows = pl.ds(c * 256, 256)
         second[rows, :] = sum_dot(
@@ -593,13 +598,20 @@
 
 
 def project(basis, krylov, next_map):
-    vmem = pl.BlockSpec(memory_space=pltpu.VMEM)
+    anywhere = pl.BlockSpec(memory_space=pltpu.HBM)
+    f32 = jnp.float32
     return pl.pallas_call(
         project_kernel,
-        out_shape=jax.ShapeDtypeStruct((NODES, K), jnp.float32),
-        in_specs=[vmem, vmem, vmem],
-        out_specs=vmem,
-        compiler_params=pltpu.CompilerParams(vmem_limit_bytes=32 * 1024 * 1024),
+        out_shape=jax.ShapeDtypeStruct((NODES, K), f32),
+        in_specs=[anywhere] * 3,
+        out_specs=pl.BlockSpec(memory_space=pltpu.VMEM),
+        scratch_shapes=[
+            pltpu.VMEM((NODES, K), f32),
+            pltpu.VMEM((NODES, K), f32),
+            pltpu.VMEM((K, 2 * K), f32),
+            pltpu.SemaphoreType.DMA((3,)),
+        ],
+        compiler_params=pltpu.CompilerParams(vmem_limit_bytes=65024 * 1024),
         cost_estimate=pl.CostEstimate(
             flops=2 * NODES * 2 * K * K * 3, bytes_accessed=4 * 2**20, transcendentals=0
         ),
@@ -610,11 +622,9 @@
 def shards(basis_start, admit, pattern, ground, capacity, ports, drive, corner_table, level_table):
     devices = lax.axis_size("gx") * lax.axis_size("gy")
     basis = basis_start.reshape(NODES, K)
-    krylov, sums = stats(
-        basis, admit, pattern, ground, capacity, ports, drive, corner_table, level_table
-    )
-    next_map, own = solve(
-        NODES * devices, ports.shape[0] * devices, sums
+    krylov, next_map, own = stats(
+        NODES * devices, ports.shape[0] * devices,
+        basis, admit, pattern, ground, capacity, ports, drive, corner_table, level_table,
     )
     swap = [(i, i ^ 1) for i in range(lax.axis_size("gx"))]
     other = lax.ppermute(own, "gx", swap)

time: 97.5 us -> 89.6 us (0.919)
  Pallas kernels: 91.2 us -> 86.3 us
  local copies, waits for them, and re-layouts: 2.63 us -> 0.01 us
    pallas_call x2 -> x1, Pallas kernels: 89.2 us -> 82.5 us  [stats(): pl.pallas_call(functools.partial(stats_kernel, nodes=nodes, drivers=drive...]
    unnamed x6 -> x2, local copies, waits for them, and re-layouts: 2.63 us -> 0.01 us
    pallas_call x1, Pallas kernels: 1.98 us -> 3.74 us  [project(): pl.pallas_call(project_kernel, out_shape=jax.ShapeDtypeStruct((NODES, K),...]
  transfers between devices with their start and end apart: 1 -> 1, of which waited for: 1 -> 1; matrix products, arithmetic and copies ran while one was open for 0% -> 0% of each run, Pallas kernels for 2% -> 4%
where the time goes in v2:
time: 89.6 us; the launch traced here: 89.5 us
  Pallas kernels  86.3 us (96%)
  waiting for transfers between devices  1.37 us (2%)
    pallas_call x1, Pallas kernels, stats(): pl.pallas_call(functools.partial(stats_kernel, nodes=nodes, drivers=drive...  82.5 us
    pallas_call x1, Pallas kernels, project(): pl.pallas_call(project_kernel, out_shape=jax.ShapeDtypeStruct((NODES, K),...  3.74 us
  transfers between devices with their start and end apart: 1, of which 1 were waited for; matrix products, arithmetic and copies ran while one was open for 0% of the time, Pallas kernels for 4%

profile of v2, /device:TPU:1, one launch (start us, length us, event | category | flops | bytes accessed | tf_op | source)
XLA Modules:
  0.0 89.5 jit_solution(4296178998217256305)
XLA Ops:
  0.6 82.5 %stats.1 = (f32[1024,256]{1,0:T(8,128)}, f32[256,512]{1,0:T(8,128)}, f32[64,512]{1,0:T(8,128)}) custom-call(f32[1024,256]{1,0:T(8,128)} %bitcast.6, f32[8,128]{1,0:T(8,128)} %admit_in.1, s32[8,128]{1,0:T(8,128)} %pattern_in.1, f32[8,128]{1,0:T(8,128)} %ground_in.1, f32[8,128]{1,0:T(8,128)} %capacity_in.1, s32[8]{0:T(128)} %ports_in.1, f32[8,64]{1,0:T(8,128)} %drive_in.1, ...), custom_call_target="tpu_custom_call" | custom-call | tf_op jit(solution)/shard_map/stats/pallas_call | solution.py:325
  83.2 0.4 collective-permute-start
  83.6 0.0 copy-start
  83.6 3.7 %project.1 = f32[1024,256]{1,0:T(8,128)} custom-call(f32[1024,256]{1,0:T(8,128)} %bitcast.7, f32[1024,256]{1,0:T(8,128)} %get-tuple-element.5.krylov_in, f32[256,512]{1,0:T(8,128)} %get-tuple-element.6.next_map_in), custom_call_target="tpu_custom_call" | custom-call | flops 805306368 | bytes 4194304 | tf_op jit(solution)/shard_map/project/pallas_call | solution.py:603
  87.3 1.4 %collective-permute-done = f32[64,512]{1,0:T(8,128)S(1)} collective-permute-done((f32[64,512]{1,0:T(8,128)}, f32[64,512]{1,0:T(8,128)S(1)}, u32[]{:S(2)}, u32[]{:S(2)}) %collective-permute-start) | collective-permute-done | bytes 131104 | tf_op jit(solution)/shard_map/ppermute | solution.py:630
  88.7 0.0 copy-done
  88.7 0.7 pad_maximum_fusion
  (1 shorter events, 0.0 us)
Async XLA Ops:
  83.2 5.5 %collective-permute-start = (f32[64,512]{1,0:T(8,128)}, f32[64,512]{1,0:T(8,128)S(1)}, u32[]{:S(2)}, u32[]{:S(2)}) collective-permute-start(f32[64,512]{1,0:T(8,128)} %get-tuple-element.7), channel_id=1, source_target_pairs={{0,16},{16,0},{32,48},{48,32},{64,80},{80,64},{96,112},{112,96},{1... | collective-permute-start | bytes 393224 | tf_op jit(solution)/shard_map/ppermute | solution.py:630
  83.6 5.1 %copy-start = (f32[64,512]{1,0:T(8,128)S(1)}, f32[64,512]{1,0:T(8,128)}, u32[]{:S(2)}) copy-start(f32[64,512]{1,0:T(8,128)} %get-tuple-element.7) | copy-start | bytes 393220

commit v3 on v2

--- a/solution.py
+++ b/solution.py
@@ -39,7 +39,6 @@
 WAVE = 512
 HALF = 256
 PIECE = 16
-SCALES = 3 * WAVE + 264
 
 
 def stats_kernel(
@@ -297,24 +296,34 @@
     start_back(3)
     start_back(2)
     start_z(4)
+    basis_first, basis_second, corner_early, corner = solver(
+        nodes, drivers, out, next_map, response, mats, low_t, cap_mat, forcing, work
+    )
+    landed(0)
+    basis_first()
     for w in (1, 3, 2):
         start_last(w)
     start_back(4)
+    for w in (1, 3, 2):
+        landed(w)
+    basis_second()
     start_last(4)
-    for w in range(WAVES):
-        landed(w)
+    corner_early()
     y_store.wait()
     for copy in started[len(halo) :]:
         copy.wait_send()
+    landed(4)
+    odd = lax.rem(gx, 2)
+    scales = []
     for kind in range(3):
+        pair = []
         for k in range(2):
             level = levels[kind, 0]
             for i in range(1, 4):
                 level = jnp.where(corners[k, kind] == i, levels[kind, i], level)
-            out[SCALES + 2 * kind + k : SCALES + 2 * kind + k + 1, :] = jnp.full((1, 128), level, jnp.float32)
-    solve_sums(
-        nodes, drivers, out, next_map, response, mats, low_t, cap_mat, forcing, work
-    )
+            pair.append(level)
+        scales.append(jnp.where(odd == 0, pair[0], pair[1]))
+    corner(*scales)
 
 
 def stats(nodes, drivers, basis, admit, pattern, ground, capacity, ports, drive, corners, levels):
@@ -410,14 +419,11 @@
     return total
 
 
-def solve_sums(
-    nodes, drivers, sums, next_map, response,
-    mats, low_t, cap_mat, forcing, work,
-):
+def solver(nodes, drivers, sums, next_map, response, mats, low_t, cap_mat, forcing, work):
     scale = 1.0 / nodes
 
-    row_id = lax.broadcasted_iota(jnp.int32, (K, K), 0)
-    col_id = lax.broadcasted_iota(jnp.int32, (K, K), 1)
+    wide_row = lax.broadcasted_iota(jnp.int32, (K, K), 0)
+    wide_col = lax.broadcasted_iota(jnp.int32, (K, K), 1)
 
     def take(w):
         start = w * WAVE
@@ -426,49 +432,21 @@
             * scale
         )
 
-    def take_pair(w, place):
+    def take_lower(w):
         both = take(w)
-        turned = both.T
+        return jnp.where(wide_row >= wide_col, both, both.T)
+
+    def take_upper(w, place):
+        both = take(w)
         at = 3 * WAVE + 256 + 2 * place
         diag = jnp.concatenate([sums[at : at + 1, :], sums[at + 1 : at + 2, :]], 1) * scale
-        lower = jnp.where(row_id >= col_id, both, turned)
-        upper = jnp.where(row_id < col_id, both, jnp.where(row_id == col_id, diag, turned))
-        return lower, upper
-
-    xx, xcx = take_pair(0, 0)
-    xy = take(1)
-    yy, xcy = take_pair(2, 1)
-    cond_tail, ycy = take_pair(4, 2)
-    mats[0, :256, :256] = xx
-    mats[0, :256, 256:] = xy
-    mats[0, 256:, 256:] = yy
-    cap_mat[:256, :256] = xcx
-    cap_mat[:256, 256:] = xcy
-    cap_mat[256:, :256] = xcy
-    cap_mat[256:, 256:] = ycy
-    k = lax.rem(lax.axis_index("gx"), 2)
-    g, ratio, gain = [
-        jnp.where(
-            k == 0,
-            sums[SCALES + 2 * i : SCALES + 2 * i + 1, 0:1],
-            sums[SCALES + 2 * i + 1 : SCALES + 2 * i + 2, 0:1],
-        )
-        for i in range(3)
-    ]
-    ratio = ratio * (1.0 / time_step)
-    mats[1, :256, :256] = g * xcy + ratio * xcx
-    mats[1, :256, 256:] = g * ycy + ratio * xcy
-    mats[1, 256:, 256:] = g * cond_tail + ratio * ycy
-    part = sums[pl.ds(3 * WAVE, 256), :] * (1.0 / math.sqrt(drivers))
-    forcing[:256, :] = part[:, :STEPS]
-    forcing[256:, :] = part[:, STEPS:]
-    for m in range(2):
-        mats[m, 256:, :256] = jnp.zeros((256, 256), jnp.float32)
+        return jnp.where(
+            wide_row < wide_col, both, jnp.where(wide_row == wide_col, diag, both.T)
+        )
 
     sub = lax.broadcasted_iota(jnp.int32, (8, 128), 0)
     row_id = lax.broadcasted_iota(jnp.int32, (BLOCK, BLOCK), 0)
     col_id = lax.broadcasted_iota(jnp.int32, (BLOCK, BLOCK), 1)
-    eye = (row_id == col_id).astype(jnp.float32)
 
     def eliminate(rows, lo, first):
         tiles = range(first, 4)
@@ -495,18 +473,18 @@
         root = lax.rsqrt(pivots)
         return [rows[first][h] * root for h in range(2)]
 
-    def factor_panel(lo):
+    def factor_panel(lo, ms):
         done = lo + 32
-        rows = [
-            [[work[m, lo + 8 * t : lo + 8 * t + 8, h * 128 : h * 128 + 128] for h in range(2)]
-             for t in range(4)]
-            for m in range(2)
-        ]
-        final = [[None] * 4, [None] * 4]
+        rows = {
+            m: [[work[m, lo + 8 * t : lo + 8 * t + 8, h * 128 : h * 128 + 128] for h in range(2)]
+                for t in range(4)]
+            for m in ms
+        }
+        final = {m: [None] * 4 for m in ms}
         for t in range(4):
-            for m in range(2):
+            for m in ms:
                 final[m][t] = eliminate(rows[m], lo, t)
-        for m in range(2):
+        for m in ms:
             panel = jnp.concatenate([jnp.concatenate(final[m][t], 1) for t in range(4)], 0)
             work[m, lo:done, :] = panel
             if done < BLOCK:
@@ -514,67 +492,118 @@
                 update = deep_dot([p[:, :BLOCK] for p in parts], parts, 0, 0)
                 work[m, done:, :] = work[m, done:, :] - update[done:, :]
 
-    def step(s, carry):
-        lo = pl.multiple_of(s * BLOCK, BLOCK)
+    def factor_blocks(places):
+        for m, place in places.items():
+            lo = pl.multiple_of(place * BLOCK, BLOCK)
+            work[m, :, :BLOCK] = mats[m, pl.ds(lo, BLOCK), pl.ds(lo, BLOCK)]
+            work[m, :, BLOCK:] = (row_id == col_id).astype(jnp.float32)
+        for p in range(BLOCK // 32):
+            factor_panel(32 * p, list(places))
+        if 0 in places:
+            lo = pl.multiple_of(places[0] * BLOCK, BLOCK)
+            low_t[pl.ds(lo, BLOCK), pl.ds(lo, BLOCK)] = jnp.where(
+                row_id <= col_id, work[0, :, :BLOCK], 0.0
+            )
+
+    def finish_block(m, i):
+        lo, hi = i * BLOCK, (i + 1) * BLOCK
+        corner = jnp.where(row_id >= col_id, work[m, :, BLOCK:], 0.0)
+        row = deep_dot(split(corner, 3), split(mats[m, lo:hi, :], 3), 1, 0)
+        if i > 0:
+            mats[m, lo:hi, :lo] = row[:, :lo]
+        mats[m, lo:hi, lo:hi] = corner
+        if i < 3:
+            mats[m, lo:hi, hi:] = jnp.zeros((BLOCK, 512 - hi), jnp.float32)
+            if m == 0:
+                low_t[lo:hi, hi:] = row[:, hi:]
+            left = [row[:, :lo]] if i > 0 else []
+            row = jnp.concatenate(left + [corner, row[:, hi:]], 1)
+            parts = split(row, 3)
+            update = deep_dot([p[:, hi:] for p in parts], parts, 0, 0)
+            if i > 0:
+                mats[m, hi:, :lo] = mats[m, hi:, :lo] - update[:, :lo]
+            mats[m, hi:, lo:hi] = -update[:, lo:hi]
+            mats[m, hi:, hi:] = mats[m, hi:, hi:] - update[:, hi:]
+
+    def basis_first():
+        low_t[...] = jnp.zeros_like(low_t)
+        mats[0, :256, :256] = take_lower(0)
         for m in range(2):
-            work[m, :, :BLOCK] = mats[m, pl.ds(lo, BLOCK), pl.ds(lo, BLOCK)]
-            work[m, :, BLOCK:] = eye
-        for p in range(BLOCK // 32):
-            factor_panel(32 * p)
-        low_t[pl.ds(lo, BLOCK), pl.ds(lo, BLOCK)] = jnp.where(
-            row_id <= col_id, work[0, :, :BLOCK], 0.0
-        )
-        for i in range(4):
-
-            @pl.when(s == i)
-            def _():
-                lo, hi = i * BLOCK, (i + 1) * BLOCK
-                for m in range(2):
-                    corner = jnp.where(row_id >= col_id, work[m, :, BLOCK:], 0.0)
-                    row = deep_dot(split(corner, 3), split(mats[m, lo:hi, :], 3), 1, 0)
-                    if i > 0:
-                        mats[m, lo:hi, :lo] = row[:, :lo]
-                    mats[m, lo:hi, lo:hi] = corner
-                    if i < 3:
-                        mats[m, lo:hi, hi:] = jnp.zeros((BLOCK, 512 - hi), jnp.float32)
-                        if m == 0:
-                            low_t[lo:hi, hi:] = row[:, hi:]
-                        left = [row[:, :lo]] if i > 0 else []
-                        row = jnp.concatenate(left + [corner, row[:, hi:]], 1)
-                        parts = split(row, 3)
-                        update = deep_dot([p[:, hi:] for p in parts], parts, 0, 0)
-                        if i > 0:
-                            mats[m, hi:, :lo] = mats[m, hi:, :lo] - update[:, :lo]
-                        mats[m, hi:, lo:hi] = -update[:, lo:hi]
-                        mats[m, hi:, hi:] = mats[m, hi:, hi:] - update[:, hi:]
-
-        return carry
-
-    low_t[...] = jnp.zeros_like(low_t)
-    lax.fori_loop(0, 4, step, 0)
-
-    next_map[...] = mats[0, 256:, :]
-    low = split(mats[1], 2)
-    half_way = sum_dot(low, split(cap_mat[...] * ratio, 2))
-    power = sum_dot(split(half_way, 2), low, 1, 1)
-    states = sum_dot(split(forcing[...] * gain, 2), low, 0, 1)
-    time = lax.broadcasted_iota(jnp.int32, (STEPS, 512), 0)
-    s = 1
-    while s < STEPS:
-        late = jnp.where(time >= s, pltpu.roll(states, s, 0), 0.0)
-        parts = split(power, 2)
-        late_parts = split(late, 2)
-        if 2 * s < STEPS:
-            both = sum_dot(
-                [jnp.concatenate([p, q], 0) for p, q in zip(parts, late_parts)], parts
-            )
-            power = both[:512]
-            states = states + both[512:]
-        else:
-            states = states + sum_dot(late_parts, parts)
-        s *= 2
-    states = sum_dot(split(states, 2), low)
-    response[...] = sum_dot(split(states, 2), split(low_t[...], 2), 1, 1)
+            mats[m, 256:, :256] = jnp.zeros((256, 256), jnp.float32)
+        factor_blocks({0: 0})
+
+    def basis_second():
+        mats[0, :256, 256:] = take(1)
+        mats[0, 256:, 256:] = take_lower(2)
+        finish_block(0, 0)
+        factor_blocks({0: 1})
+        finish_block(0, 1)
+
+    def corner_early():
+        xcx, xcy = take_upper(0, 0), take_upper(2, 1)
+        cap_mat[:256, :256] = xcx
+        cap_mat[:256, 256:] = xcy
+        cap_mat[256:, :256] = xcy
+        part = sums[pl.ds(3 * WAVE, 256), :] * (1.0 / math.sqrt(drivers))
+        forcing[:256, :] = part[:, :STEPS]
+        forcing[256:, :] = part[:, STEPS:]
+
+    def corner(g, ratio, gain):
+        ratio = ratio * (1.0 / time_step)
+        xcx, xcy = cap_mat[:256, :256], cap_mat[:256, 256:]
+        cond_tail, ycy = take_lower(4), take_upper(4, 2)
+        cap_mat[256:, 256:] = ycy
+        mats[1, :256, :256] = g * xcy + ratio * xcx
+        mats[1, :256, 256:] = g * ycy + ratio * xcy
+        mats[1, 256:, 256:] = g * cond_tail + ratio * ycy
+
+        def both(s, carry):
+            factor_blocks({0: s + 2, 1: s})
+            for i in range(2):
+
+                @pl.when(s == i)
+                def _():
+                    finish_block(0, i + 2)
+                    finish_block(1, i)
+
+            return carry
+
+        def alone(s, carry):
+            factor_blocks({1: s})
+            for i in range(2, 4):
+
+                @pl.when(s == i)
+                def _():
+                    finish_block(1, i)
+
+            return carry
+
+        lax.fori_loop(0, 2, both, 0)
+        lax.fori_loop(2, 4, alone, 0)
+        next_map[...] = mats[0, 256:, :]
+        low = split(mats[1], 2)
+        half_way = sum_dot(low, split(cap_mat[...] * ratio, 2))
+        power = sum_dot(split(half_way, 2), low, 1, 1)
+        states = sum_dot(split(forcing[...] * gain, 2), low, 0, 1)
+        time = lax.broadcasted_iota(jnp.int32, (STEPS, 512), 0)
+        s = 1
+        while s < STEPS:
+            late = jnp.where(time >= s, pltpu.roll(states, s, 0), 0.0)
+            parts = split(power, 2)
+            late_parts = split(late, 2)
+            if 2 * s < STEPS:
+                both = sum_dot(
+                    [jnp.concatenate([p, q], 0) for p, q in zip(parts, late_parts)], parts
+                )
+                power = both[:512]
+                states = states + both[512:]
+            else:
+                states = states + sum_dot(late_parts, parts)
+            s *= 2
+        states = sum_dot(split(states, 2), low)
+        response[...] = sum_dot(split(states, 2), split(low_t[...], 2), 1, 1)
+
+    return basis_first, basis_second, corner_early, corner
 
 
 def project_kernel(basis_in, krylov_in, next_map_in, second, basis, krylov, next_map, load_sem):

time: 89.6 us -> 87.8 us (0.980)
  Pallas kernels: 86.3 us -> 85 us
    pallas_call x1, Pallas kernels: 82.5 us -> 81.2 us  [stats(): pl.pallas_call(functools.partial(stats_kernel, nodes=nodes, drivers=drive...]
where the time goes in v3:
time: 87.8 us; the launch traced here: 87.6 us
  Pallas kernels  85 us (97%)
    pallas_call x1, Pallas kernels, stats(): pl.pallas_call(functools.partial(stats_kernel, nodes=nodes, drivers=drive...  81.2 us
    pallas_call x1, Pallas kernels, project(): pl.pallas_call(project_kernel, out_shape=jax.ShapeDtypeStruct((NODES, K),...  3.74 us
  transfers between devices with their start and end apart: 1, of which 1 were waited for; matrix products, arithmetic and copies ran while one was open for 0% of the time, Pallas kernels for 4%

profile of v3, /device:TPU:1, one launch (start us, length us, event | category | flops | bytes accessed | tf_op | source)
XLA Modules:
  0.0 87.6 jit_solution(4279356606620347470)
XLA Ops:
  0.6 81.2 %stats.1 = (f32[1024,256]{1,0:T(8,128)}, f32[256,512]{1,0:T(8,128)}, f32[64,512]{1,0:T(8,128)}) custom-call(f32[1024,256]{1,0:T(8,128)} %bitcast.6, f32[8,128]{1,0:T(8,128)} %admit_in.1, s32[8,128]{1,0:T(8,128)} %pattern_in.1, f32[8,128]{1,0:T(8,128)} %ground_in.1, f32[8,128]{1,0:T(8,128)} %capacity_in.1, s32[8]{0:T(128)} %ports_in.1, f32[8,64]{1,0:T(8,128)} %drive_in.1, ...), custom_call_target="tpu_custom_call" | custom-call | tf_op jit(solution)/shard_map/stats/pallas_call | solution.py:334
  81.9 0.6 collective-permute-start
  82.5 0.0 copy-start
  82.5 3.7 %project.1 = f32[1024,256]{1,0:T(8,128)} custom-call(f32[1024,256]{1,0:T(8,128)} %bitcast.7, f32[1024,256]{1,0:T(8,128)} %get-tuple-element.5.krylov_in, f32[256,512]{1,0:T(8,128)} %get-tuple-element.6.next_map_in), custom_call_target="tpu_custom_call" | custom-call | flops 805306368 | bytes 4194304 | tf_op jit(solution)/shard_map/project/pallas_call | solution.py:632
  86.2 0.7 collective-permute-done
  86.9 0.0 copy-done
  86.9 0.7 pad_maximum_fusion
  (1 shorter events, 0.0 us)
Async XLA Ops:
  81.9 5.0 %collective-permute-start = (f32[64,512]{1,0:T(8,128)}, f32[64,512]{1,0:T(8,128)S(1)}, u32[]{:S(2)}, u32[]{:S(2)}) collective-permute-start(f32[64,512]{1,0:T(8,128)} %get-tuple-element.7), channel_id=1, source_target_pairs={{0,16},{16,0},{32,48},{48,32},{64,80},{80,64},{96,112},{112,96},{1... | collective-permute-start | bytes 393224 | tf_op jit(solution)/shard_map/ppermute | solution.py:659
  82.5 4.4 %copy-start = (f32[64,512]{1,0:T(8,128)S(1)}, f32[64,512]{1,0:T(8,128)}, u32[]{:S(2)}) copy-start(f32[64,512]{1,0:T(8,128)} %get-tuple-element.7) | copy-start | bytes 393220

commit v4 on v3

--- a/solution.py
+++ b/solution.py
@@ -456,12 +456,18 @@
             for t in tiles
         }
         pivots = None
+
+        def spread(k, row):
+            return jnp.broadcast_to(cols[first][k][row : row + 1, :], (8, 128))
+
+        pivot = spread(0, 0)
         for i in range(8):
-            pivot = jnp.broadcast_to(cols[first][i][i : i + 1, :], (8, 128))
             inverse = 1.0 / pivot
             pivots = pivot if pivots is None else jnp.where(sub == i, pivot, pivots)
-            below = {t: cols[t][i] * inverse for t in tiles}
-            below[first] = jnp.where(sub > i, below[first], 0.0)
+            if i < 7:
+                ahead = spread(i + 1, i + 1) - (spread(i, i + 1) * spread(i + 1, i)) * inverse
+            below = {t: cols[t][i] * inverse for t in tiles if t != first}
+            below[first] = jnp.where(sub > i, cols[first][i], 0.0) * inverse
             for k in range(i + 1, 8):
                 top = jnp.broadcast_to(cols[first][k][i : i + 1, :], (8, 128))
                 for t in tiles:
@@ -470,6 +476,7 @@
                 top = jnp.broadcast_to(rows[first][h][i : i + 1, :], (8, 128))
                 for t in tiles:
                     rows[t][h] = rows[t][h] - below[t] * top
+            pivot = ahead
         root = lax.rsqrt(pivots)
         return [rows[first][h] * root for h in range(2)]
 
@@ -587,19 +594,20 @@
         states = sum_dot(split(forcing[...] * gain, 2), low, 0, 1)
         time = lax.broadcasted_iota(jnp.int32, (STEPS, 512), 0)
         s = 1
-        while s < STEPS:
+        while s < 16:
             late = jnp.where(time >= s, pltpu.roll(states, s, 0), 0.0)
             parts = split(power, 2)
-            late_parts = split(late, 2)
-            if 2 * s < STEPS:
-                both = sum_dot(
-                    [jnp.concatenate([p, q], 0) for p, q in zip(parts, late_parts)], parts
-                )
-                power = both[:512]
-                states = states + both[512:]
-            else:
-                states = states + sum_dot(late_parts, parts)
+            both = sum_dot(
+                [jnp.concatenate([p, q], 0) for p, q in zip(parts, split(late, 2))], parts
+            )
+            power = both[:512]
+            states = states + both[512:]
             s *= 2
+        parts = split(power, 2)
+        runs = [states[:s]]
+        for first in range(s, STEPS, s):
+            runs.append(states[first : first + s] + sum_dot(split(runs[-1], 2), parts))
+        states = jnp.concatenate(runs, 0)
         states = sum_dot(split(states, 2), low)
         response[...] = sum_dot(split(states, 2), split(low_t[...], 2), 1, 1)
 

time: 87.8 us -> 86.4 us (0.984)
  Pallas kernels: 85 us -> 83.6 us
    pallas_call x1, Pallas kernels: 81.2 us -> 79.8 us  [stats(): pl.pallas_call(functools.partial(stats_kernel, nodes=nodes, drivers=drive...]
where the time goes in v4:
time: 86.4 us; the launch traced here: 86.2 us
  Pallas kernels  83.6 us (97%)
    pallas_call x1, Pallas kernels, stats(): pl.pallas_call(functools.partial(stats_kernel, nodes=nodes, drivers=drive...  79.8 us
    pallas_call x1, Pallas kernels, project(): pl.pallas_call(project_kernel, out_shape=jax.ShapeDtypeStruct((NODES, K),...  3.74 us
  transfers between devices with their start and end apart: 1, of which 1 were waited for; matrix products, arithmetic and copies ran while one was open for 0% of the time, Pallas kernels for 4%

profile of v4, /device:TPU:1, one launch (start us, length us, event | category | flops | bytes accessed | tf_op | source)
XLA Modules:
  0.0 86.2 jit_solution(9772500054422077653)
XLA Ops:
  0.6 79.8 %stats.1 = (f32[1024,256]{1,0:T(8,128)}, f32[256,512]{1,0:T(8,128)}, f32[64,512]{1,0:T(8,128)}) custom-call(f32[1024,256]{1,0:T(8,128)} %bitcast.6, f32[8,128]{1,0:T(8,128)} %admit_in.1, s32[8,128]{1,0:T(8,128)} %pattern_in.1, f32[8,128]{1,0:T(8,128)} %ground_in.1, f32[8,128]{1,0:T(8,128)} %capacity_in.1, s32[8]{0:T(128)} %ports_in.1, f32[8,64]{1,0:T(8,128)} %drive_in.1, ...), custom_call_target="tpu_custom_call" | custom-call | tf_op jit(solution)/shard_map/stats/pallas_call | solution.py:334
  80.5 0.6 collective-permute-start
  81.1 0.0 copy-start
  81.1 3.7 %project.1 = f32[1024,256]{1,0:T(8,128)} custom-call(f32[1024,256]{1,0:T(8,128)} %bitcast.7, f32[1024,256]{1,0:T(8,128)} %get-tuple-element.5.krylov_in, f32[256,512]{1,0:T(8,128)} %get-tuple-element.6.next_map_in), custom_call_target="tpu_custom_call" | custom-call | flops 805306368 | bytes 4194304 | tf_op jit(solution)/shard_map/project/pallas_call | solution.py:640
  84.8 0.7 collective-permute-done
  85.5 0.0 copy-done
  85.5 0.7 pad_maximum_fusion
  (1 shorter events, 0.0 us)
Async XLA Ops:
  80.5 5.0 %collective-permute-start = (f32[64,512]{1,0:T(8,128)}, f32[64,512]{1,0:T(8,128)S(1)}, u32[]{:S(2)}, u32[]{:S(2)}) collective-permute-start(f32[64,512]{1,0:T(8,128)} %get-tuple-element.7), channel_id=1, source_target_pairs={{0,16},{16,0},{32,48},{48,32},{64,80},{80,64},{96,112},{112,96},{1... | collective-permute-start | bytes 393224 | tf_op jit(solution)/shard_map/ppermute | solution.py:667
  81.1 4.4 %copy-start = (f32[64,512]{1,0:T(8,128)S(1)}, f32[64,512]{1,0:T(8,128)}, u32[]{:S(2)}) copy-start(f32[64,512]{1,0:T(8,128)} %get-tuple-element.7) | copy-start | bytes 393220
